TPU v7x, 32 devices: a whole 2x2x4 slice. The times are simulated.
32 devices in a mesh: groups: 2 (over y), traj: 4 (over z), fsdp: 2 (over x), sub: 2 (over core).
Axes of the slice: x: 2, y: 2, z: 4, core: 2. Of those that a mesh axis runs over, the one named last changes fastest.
Arguments:
- activations: bfloat16 [4096, 8192], P(('groups', 'traj', 'fsdp', 'sub')), parts along dimension 0, may hold values from -6 to 6
- out_grads: bfloat16 [4096, 8192], P(('groups', 'traj', 'fsdp', 'sub')), parts along dimension 0, may hold values from -6 to 6
- segments: int32 [32, 128], P(('groups', 'traj', 'fsdp', 'sub')), parts along dimension 0, may hold values from 0 to 7, never falling along the last dimension, each value on 1 to 64 neighbouring positions
- loss_mask: int32 [32, 128], P(('groups', 'traj', 'fsdp', 'sub')), parts along dimension 0, may hold values 0 or 1
- proj_in: bfloat16 [64, 8192], P(None, ('fsdp', 'sub')), may hold values from -0.0625 to 0.0625
- proj_out: bfloat16 [64, 8192], P(None, ('fsdp', 'sub')), may hold values from -0.0625 to 0.0625
- queries: float32 [128, 4096], P(('groups', 'traj')), parts along dimension 0, may hold values from -0.375 to 0.375
Outputs:
- scores: float32 [128, 128], P('groups', ('traj', 'fsdp', 'sub')), parts along dimension 0
There are 2 independent parts, one for each index of `groups`. A program takes and returns all parts, laid end to end along the dimension named above; an argument that names none is the same for every part. Nothing has to cross between parts.
Inputs may be any that keep to these rules, and one draw needn't show every extreme that they name: `segments`: within a device's row of 128 tokens segment numbers never fall; each of the 8 trajectories holds 1 to 64 tokens and one holds exactly 64.
All inputs are finite; a program needn't handle non-finite values. No bound on the sum of `loss_mask` on one device may be relied on, other than what follows from the above.
Results may differ from a plain program's by a relative error of at most 0.0003.
Values may be sent and summed in bfloat16 or wider, within the bound.
No kernel may reach another device: no remote copies, remote signals or barrier semaphores. Data moves between devices by JAX's collectives and lax.ppermute only.
A program may use at most 64 MiB of HBM per device.

v0:
```python
import jax
import jax.numpy as jnp
from jax import lax
from jax.sharding import PartitionSpec as P

TRAJ_DEV = 8


def body(activations, out_grads, segments, loss_mask, proj_in, proj_out, queries):
    highest = lax.Precision.HIGHEST
    proj_rank = proj_in.shape[0]
    tok_count = activations.shape[0]
    contract = (((1,), (1,)), ((), ()))
    in_part = lax.dot_general(
        activations,
        lax.all_gather(proj_in, ("fsdp", "sub"), axis=1, tiled=True),
        contract,
        preferred_element_type=jnp.float32,
    )
    out_part = lax.dot_general(
        out_grads,
        lax.all_gather(proj_out, ("fsdp", "sub"), axis=1, tiled=True),
        contract,
        preferred_element_type=jnp.float32,
    )
    segment = segments[0]
    one_hot = (segment[:, None] == jnp.arange(TRAJ_DEV, dtype=jnp.int32)[None, :]).astype(
        jnp.float32
    )
    mask_float = loss_mask[0].astype(jnp.float32)
    counts = jnp.dot(mask_float, one_hot, precision=highest)
    weight = mask_float * jnp.dot(one_hot, 1.0 / jnp.maximum(counts, 1.0), precision=highest)
    outer_rows = (out_part[:, :, None] * in_part[:, None, :]).reshape(
        tok_count, proj_rank * proj_rank
    )
    train_grads = jnp.dot((one_hot * weight[:, None]).T, outer_rows, precision=highest)
    return lax.dot_general(
        lax.all_gather(queries, "traj", axis=0, tiled=True),
        train_grads,
        contract,
        precision=highest,
        preferred_element_type=jnp.float32,
    )


def solution(mesh):
    placed = (
        P(("groups", "traj", "fsdp", "sub"), None),
        P(("groups", "traj", "fsdp", "sub"), None),
        P(("groups", "traj", "fsdp", "sub"), None),
        P(("groups", "traj", "fsdp", "sub"), None),
        P(None, ("fsdp", "sub")),
        P(None, ("fsdp", "sub")),
        P(("groups", "traj"), None),
    )
    return jax.shard_map(
        body,
        mesh=mesh,
        in_specs=placed,
        out_specs=P("groups", ("traj", "fsdp", "sub")),
        check_vma=False,
    )
```

profile of v0, /device:TPU:0, one launch (start us, length us, event | category | flops | bytes accessed | tf_op | source)
XLA Modules:
  0.0 85.5 jit_solution(5513097468624282175)
XLA Ops:
  6.5 0.0 copy-start
  6.5 0.0 all-gather.4.cloned.1.call-start
  6.5 0.7 all-gather.4.cloned.1.call-update
  7.3 0.0 all-gather.6.cloned.1.call-start
  7.3 0.7 all-gather.6.cloned.1.call-update
  8.0 0.0 all-gather.8.cloned.1.call-start
  8.1 0.7 all-gather.8.cloned.1.call-update
  8.7 0.9 %fusion.3 = f32[8,1]{0,1:T(1,128)S(1)} fusion(s32[128]{0:T(128)} %bitcast.32, s32[1,128]{1,0:T(1,128)} %param.10), kind=kOutput, calls=%fused_computation.6 | convolution fusion | flops 13456 | bytes 1056 | tf_op jit(solution)/shard_map/dot_general | solution.py:31
  9.6 0.9 %fusion = f32[128]{0:T(128)S(1)} fusion(f32[8,1]{0,1:T(1,128)S(1)} %fusion.3, s32[128]{0:T(128)} %bitcast.33, s32[1,128]{1,0:T(1,128)} %param.10), kind=kOutput, calls=%fused_computation.2 | convolution fusion | flops 13568 | bytes 1568 | tf_op jit(solution)/shard_map/dot_general | solution.py:32
  10.5 17.9 %all-gather.4.cloned.1.call-done = bf16[64,8192]{1,0:T(8,128)(2,1)} async-done(((bf16[64,2048]{1,0:T(8,128)(2,1)}), bf16[64,8192]{1,0:T(8,128)(2,1)}) %all-gather.4.cloned.1.call-update) | async-done | bytes 1048592 | tf_op jit(solution)/shard_map/all_gather | solution.py:22
  28.4 0.0 copy-done
  28.4 2.1 %fusion.14 = f32[128,64]{0,1:T(8,128)S(1)} fusion(bf16[128,8192]{1,0:T(8,128)(2,1)S(1)} %copy-done, bf16[64,8192]{1,0:T(8,128)(2,1)} %all-gather.4.cloned.1.call-done), kind=kOutput, calls=%fused_computation.19 | convolution fusion | flops 134217728 | bytes 3178496 | tf_op jit(solution)/shard_map/dot_general | solution.py:20
  30.4 0.0 copy-start.1
  30.5 16.2 %all-gather.6.cloned.1.call-done = bf16[64,8192]{1,0:T(8,128)(2,1)} async-done(((bf16[64,2048]{1,0:T(8,128)(2,1)}), bf16[64,8192]{1,0:T(8,128)(2,1)}) %all-gather.6.cloned.1.call-update) | async-done | bytes 1048592 | tf_op jit(solution)/shard_map/all_gather | solution.py:16
  46.7 2.7 %fusion.15 = f32[128,64]{0,1:T(8,128)S(1)} fusion(bf16[128,8192]{1,0:T(8,128)(2,1)} %param.7, bf16[64,8192]{1,0:T(8,128)(2,1)} %all-gather.6.cloned.1.call-done), kind=kOutput, calls=%fused_computation.20 | convolution fusion | flops 134217728 | bytes 3178496 | tf_op jit(solution)/shard_map/dot_general | solution.py:14
  49.4 0.3 broadcast_multiply_fusion
  49.7 0.0 copy-done.1
  49.7 1.9 %fusion.4 = f32[8,4096]{1,0:T(8,128)S(1)} fusion(f32[128,4096]{0,1:T(8,128)S(1)} %bitcast.31, f32[128]{0:T(128)S(1)} %fusion, s32[128]{0:T(128)S(1)} %bitcast.34), kind=kOutput, calls=%fused_computation.8 | convolution fusion | flops 50333696 | bytes 2229248 | tf_op jit(solution)/shard_map/dot_general | solution.py:36
  51.5 24.7 %all-gather.8.cloned.1.call-done = f32[64,4096]{1,0:T(8,128)} async-done(((f32[16,4096]{1,0:T(8,128)}), f32[64,4096]{1,0:T(8,128)}) %all-gather.8.cloned.1.call-update) | async-done | bytes 1048592 | tf_op jit(solution)/shard_map/all_gather | solution.py:38
  76.2 2.7 %convolution_bitcast_fusion = f32[64,8]{0,1:T(8,128)} fusion(f32[8,4096]{1,0:T(8,128)S(1)} %fusion.4, f32[64,4096]{1,0:T(8,128)} %all-gather.8.cloned.1.call-done), kind=kOutput, calls=%fused_computation | convolution fusion | flops 25165824 | bytes 1181696 | tf_op jit(solution)/shard_map/dot_general | solution.py:37
Async XLA Ops:
  6.5 21.8 %copy-start = (bf16[128,8192]{1,0:T(8,128)(2,1)S(1)}, bf16[128,8192]{1,0:T(8,128)(2,1)}, u32[]{:S(2)}) copy-start(bf16[128,8192]{1,0:T(8,128)(2,1)} %param.8) | copy-start | bytes 6291460
  6.5 21.8 %all-gather.4.cloned.1.call-start = ((), (), s32[]{:S(2)}) async-start(), calls=%async_computation | async-start | bytes 1310720 | tf_op jit(solution)/shard_map/all_gather | solution.py:22
  7.3 39.4 %all-gather.6.cloned.1.call-start = ((), (), s32[]{:S(2)}) async-start(), calls=%async_computation.1 | async-start | bytes 1310720 | tf_op jit(solution)/shard_map/all_gather | solution.py:16
  8.0 68.2 %all-gather.8.cloned.1.call-start = ((), (), s32[]{:S(2)}) async-start(), calls=%async_computation.2 | async-start | bytes 1310720 | tf_op jit(solution)/shard_map/all_gather | solution.py:38
  30.4 19.2 %copy-start.1 = (s32[1,128]{1,0:T(1,128)S(1)}, s32[1,128]{1,0:T(1,128)}, u32[]{:S(2)}) copy-start(s32[1,128]{1,0:T(1,128)} %param.9) | copy-start | bytes 1540
Sparse Core Ops, SparseCore 0:
  8.9 19.4 all-gather.3
  29.9 16.7 all-gather.5
  48.3 27.9 all-gather.7
where the time goes:
time: 85.7 us; the launch traced here: 85.5 us
  waiting for transfers between devices  60.9 us (71%)
  between operations  13.1 us (15%)
  matrix products  11.1 us (13%)
    all_gather x1, waiting for transfers between devices, body(): lax.all_gather(queries, 'traj', axis=0, tiled=True)  24.7 us
    all_gather x1, waiting for transfers between devices, body(): lax.all_gather(proj_out, ('fsdp', 'sub'), axis=1, tiled=True)  17.9 us
    all_gather x1, waiting for transfers between devices, body(): lax.all_gather(proj_in, ('fsdp', 'sub'), axis=1, tiled=True)  16.2 us
    dot_general x1, matrix products, body(): lax.dot_general(lax.all_gather(queries, 'traj', axis=0, tiled=True), trai...  2.74 us
    dot_general x1, matrix products, body(): lax.dot_general(activations, lax.all_gather(proj_in, ('fsdp', 'sub'), axi...  2.7 us
    unnamed x3, waiting for transfers between devices  2.09 us
    dot_general x1, matrix products, body(): lax.dot_general(out_grads, lax.all_gather(proj_out, ('fsdp', 'sub'), axis...  2.07 us
    dot_general x1, matrix products, body(): jnp.dot((one_hot * weight[:, None]).T, outer_rows, precision=highest)  1.87 us
  transfers between devices with their start and end apart: 3, of which 3 were waited for; matrix products, arithmetic and copies ran while one was open for 10% of the time, Pallas kernels for 0%

commit v1 on v0

v1 whole, which is shorter than its diff:
```python
import jax
import jax.numpy as jnp
from jax import lax
from jax.experimental import pallas as pl
from jax.experimental.pallas import tpu as pltpu
from jax.sharding import PartitionSpec as P

TRAJ_DEV = 8
NT = (((1,), (1,)), ((), ()))
HIGHEST = lax.Precision.HIGHEST
ANY = pl.BlockSpec(memory_space=pl.ANY)
VMEM = pl.BlockSpec(memory_space=pltpu.VMEM)


def dot_nt(a, b, precision=None):
    return lax.dot_general(
        a, b, NT, precision=precision, preferred_element_type=jnp.float32
    )


def project(owners, toks, projs, base):
    rank, width = projs[0].shape
    count = toks.shape[0]

    def kernel(*refs):
        owner_ref, tok_hbm = refs[:2]
        proj_hbm = refs[2 : 2 + len(projs)]
        base_ref = refs[2 + len(projs)] if base is not None else None
        out_ref, tok, proj, tok_sem, proj_sem = refs[-5:]
        copies = []
        for i in range(len(projs)):
            columns = pl.ds(pl.multiple_of(owner_ref[i] * width, 128), width)
            pair = (
                pltpu.make_async_copy(tok_hbm.at[:, columns], tok.at[i], tok_sem.at[i]),
                pltpu.make_async_copy(proj_hbm[i], proj.at[i], proj_sem.at[i]),
            )
            for copy in pair:
                copy.start()
            copies.append(pair)
        total = None
        for i, pair in enumerate(copies):
            for copy in pair:
                copy.wait()
            part = dot_nt(proj[i], tok[i])
            total = part if total is None else total + part
        out_ref[...] = total if base is None else total + base_ref[...]

    return pl.pallas_call(
        kernel,
        out_shape=jax.ShapeDtypeStruct((rank, count), jnp.float32),
        in_specs=[pl.BlockSpec(memory_space=pltpu.SMEM), ANY]
        + [ANY] * len(projs)
        + ([VMEM] if base is not None else []),
        out_specs=VMEM,
        scratch_shapes=[
            pltpu.VMEM((len(projs), count, width), toks.dtype),
            pltpu.VMEM((len(projs), rank, width), toks.dtype),
            pltpu.SemaphoreType.DMA((len(projs),)),
            pltpu.SemaphoreType.DMA((len(projs),)),
        ],
        compiler_params=pltpu.CompilerParams(vmem_limit_bytes=32 << 20),
        cost_estimate=pl.CostEstimate(
            flops=2 * rank * count * width * len(projs),
            bytes_accessed=2 * (count + rank) * width * len(projs),
            transcendentals=0,
        ),
    )(owners, toks, *projs, *([base] if base is not None else []))


def finish(in_t, out_t, segments, loss_mask, queries):
    rank, count = in_t.shape
    asked = queries.shape[0]

    def kernel(in_ref, out_ref, seg_ref, mask_ref, q_ref, score_ref):
        own = seg_ref[...] == lax.broadcasted_iota(jnp.int32, (TRAJ_DEV, count), 0)
        masked = jnp.where(own, mask_ref[...].astype(jnp.float32), 0.0)
        counts = jnp.sum(masked, axis=1, keepdims=True)
        weight = masked * (1.0 / jnp.maximum(counts, 1.0))
        left = (out_ref[...][:, None, :] * weight[None]).reshape(rank * TRAJ_DEV, count)
        twice = jnp.concatenate([in_ref[...], in_ref[...]], axis=0)
        grads = dot_nt(left, twice, HIGHEST).reshape(rank // 2, 2, TRAJ_DEV, 2 * rank)
        low = lax.broadcasted_iota(jnp.int32, (TRAJ_DEV, 2 * rank), 1) < rank
        flat = jnp.concatenate(
            [jnp.where(low, grads[p, 0], grads[p, 1]) for p in range(rank // 2)], axis=1
        )
        score_ref[...] = dot_nt(flat, q_ref[...], HIGHEST)

    return pl.pallas_call(
        kernel,
        out_shape=jax.ShapeDtypeStruct((TRAJ_DEV, asked), jnp.float32),
        in_specs=[VMEM] * 5,
        out_specs=VMEM,
        compiler_params=pltpu.CompilerParams(vmem_limit_bytes=48 << 20),
        cost_estimate=pl.CostEstimate(
            flops=12 * TRAJ_DEV * rank * rank * (count + asked),
            bytes_accessed=4 * asked * rank * rank,
            transcendentals=0,
        ),
    )(in_t, out_t, segments, loss_mask, queries)


def gather_queries(queries, core, groups_of):
    if groups_of > 4:
        return lax.all_gather(queries, "traj", axis=0, tiled=True)
    half = queries.shape[0] // 2
    mine = lax.dynamic_slice_in_dim(queries, core * half, half, 0)
    swap = [(0, 1), (1, 0)]
    at = lax.axis_index("traj")
    out = jnp.zeros((groups_of,) + queries.shape, queries.dtype)
    out = lax.dynamic_update_slice(out, queries[None], (at, 0, 0))
    for d in range(1, groups_of):
        got = lax.ppermute(mine, "traj", [(i, (i + d) % groups_of) for i in range(groups_of)])
        other = lax.ppermute(got, "sub", swap)
        both = jnp.where(
            core == 0,
            jnp.concatenate([got, other], 0),
            jnp.concatenate([other, got], 0),
        )
        out = lax.dynamic_update_slice(
            out, both[None], ((at - d) % groups_of, 0, 0)
        )
    return out.reshape(-1, queries.shape[1])


def body(sizes, activations, out_grads, segments, loss_mask, proj_in, proj_out, queries):
    chips = sizes["fsdp"]
    x, core = lax.axis_index("fsdp"), lax.axis_index("sub")
    swap = [(0, 1), (1, 0)]

    def to_core(a):
        return lax.ppermute(a, "sub", swap)

    def from_chip(a, d):
        return lax.ppermute(a, "fsdp", [((i + d) % chips, i) for i in range(chips)])

    far_in = [from_chip(proj_in, d) for d in range(1, chips)]
    far_out = [from_chip(proj_out, d) for d in range(1, chips)]
    near = jnp.stack([2 * x + core, 2 * x + 1 - core]).astype(jnp.int32)
    far = jnp.stack(
        [2 * ((x + d) % chips) + c for d in range(1, chips) for c in (core, 1 - core)]
    ).astype(jnp.int32)
    in_t = project(near, activations, [proj_in, to_core(proj_in)], None)
    out_t = project(near, out_grads, [proj_out, to_core(proj_out)], None)
    in_t = project(far, activations, [b for a in far_in for b in (a, to_core(a))], in_t)
    out_t = project(far, out_grads, [b for a in far_out for b in (a, to_core(a))], out_t)
    everyone = gather_queries(queries, core, sizes["traj"])
    return finish(in_t, out_t, segments, loss_mask, everyone).T


def solution(mesh):
    placed = (
        P(("groups", "traj", "fsdp", "sub"), None),
        P(("groups", "traj", "fsdp", "sub"), None),
        P(("groups", "traj", "fsdp", "sub"), None),
        P(("groups", "traj", "fsdp", "sub"), None),
        P(None, ("fsdp", "sub")),
        P(None, ("fsdp", "sub")),
        P(("groups", "traj"), None),
    )
    sizes = dict(mesh.shape)

    def program(*arrays):
        return body(sizes, *arrays)

    return jax.shard_map(
        program,
        mesh=mesh,
        in_specs=placed,
        out_specs=P("groups", ("traj", "fsdp", "sub")),
        check_vma=False,
    )
```

time: 85.7 us -> 36.1 us (0.42)
  waiting for transfers between devices: 60.9 us -> 9.79 us
  between operations: 13.1 us -> 0.18 us
  starting transfers between devices: 0.08 us -> 11.4 us
  matrix products: 11.1 us -> 0 us
  Pallas kernels: 0 us -> 8.97 us
  other arithmetic: 0.26 us -> 3.3 us
  local copies, waits for them, and re-layouts: 0.01 us -> 2.13 us
    all_gather x3 -> x0, waiting for transfers between devices: 58.8 us -> none  [the longest x1 24.7 us: body(): lax.all_gather(queries, 'traj', axis=0, tiled=True)]
    ppermute x0 -> x12, starting transfers between devices: none -> 11.4 us  [the longest x3 7.01 us: gather_queries(): lax.ppermute(mine, 'traj', [(i, (i + d) % groups_of) for i in range(group...]
    dot_general x6 -> x0, matrix products: 11.1 us -> none  [the longest x1 2.74 us: body(): lax.dot_general(lax.all_gather(queries, 'traj', axis=0, tiled=True), trai...]
    ppermute x0 -> x12, waiting for transfers between devices: none -> 9.79 us  [the longest x2 5.34 us: from_chip(): return lax.ppermute(a, 'fsdp', [((i + d) % chips, i) for i in range(chips)])]
    pallas_call x0 -> x5, Pallas kernels: none -> 8.97 us  [the longest x4 6.68 us: project(): pl.pallas_call(kernel, out_shape=jax.ShapeDtypeStruct((rank, count), jnp....]
    dynamic_update_slice x0 -> x3, other arithmetic: none -> 3.15 us  [gather_queries(): lax.dynamic_update_slice(out, both[None], ((at - d) % groups_of, 0, 0))]
    unnamed x3 -> x0, waiting for transfers between devices: 2.09 us -> none
    dynamic_slice x0 -> x1, local copies, waits for them, and re-layouts: none -> 1.06 us  [gather_queries(): mine = lax.dynamic_slice_in_dim(queries, core * half, half, 0)]
  transfers between devices with their start and end apart: 3 -> 12, of which waited for: 3 -> 3; matrix products, arithmetic and copies ran while one was open for 10% -> 12% of each run, Pallas kernels for 0% -> 15%
where the time goes in v1:
time: 36.1 us; the launch traced here: 35.8 us
  starting transfers between devices  11.4 us (32%)
  waiting for transfers between devices  9.79 us (27%)
  Pallas kernels  8.97 us (25%)
  other arithmetic  3.3 us (9%)
  local copies, waits for them, and re-layouts  2.13 us (6%)
    ppermute x3, starting transfers between devices, gather_queries(): lax.ppermute(mine, 'traj', [(i, (i + d) % groups_of) for i in range(group...  7.01 us
    pallas_call x4, Pallas kernels, project(): pl.pallas_call(kernel, out_shape=jax.ShapeDtypeStruct((rank, count), jnp....  6.68 us
    ppermute x2, waiting for transfers between devices, from_chip(): return lax.ppermute(a, 'fsdp', [((i + d) % chips, i) for i in range(chips)])  5.34 us
    ppermute x3, waiting for transfers between devices, gather_queries(): lax.ppermute(mine, 'traj', [(i, (i + d) % groups_of) for i in range(group...  4.44 us
    dynamic_update_slice x3, other arithmetic, gather_queries(): lax.dynamic_update_slice(out, both[None], ((at - d) % groups_of, 0, 0))  3.15 us
    ppermute x2, starting transfers between devices, from_chip(): return lax.ppermute(a, 'fsdp', [((i + d) % chips, i) for i in range(chips)])  3.05 us
    pallas_call x1, Pallas kernels, finish(): pl.pallas_call(kernel, out_shape=jax.ShapeDtypeStruct((TRAJ_DEV, asked),...  2.29 us
    dynamic_slice x1, local copies, waits for them, and re-layouts, gather_queries(): mine = lax.dynamic_slice_in_dim(queries, core * half, half, 0)  1.06 us
  transfers between devices with their start and end apart: 12, of which 3 were waited for; matrix products, arithmetic and copies ran while one was open for 12% of the time, Pallas kernels for 15%

profile of v1, /device:TPU:0, one launch (start us, length us, event | category | flops | bytes accessed | tf_op | source)
XLA Modules:
  0.0 35.8 jit_solution(17459455548262486499)
XLA Ops:
  0.0 1.1 %constant_dynamic-slice_fusion = f32[8,4096]{1,0:T(8,128)S(1)} fusion(f32[16,4096]{1,0:T(8,128)} %param.13, s32[]{:T(128)S(6)} %select_n.76), kind=kLoop, calls=%fused_computation.7 | loop fusion | bytes 262148 | tf_op jit(solution)/shard_map/dynamic_slice | solution.py:106
  1.1 3.1 %collective-permute-start.6 = (f32[8,4096]{1,0:T(8,128)S(1)}, f32[8,4096]{1,0:T(8,128)}, u32[]{:S(2)}, u32[]{:S(2)}) collective-permute-start(f32[8,4096]{1,0:T(8,128)S(1)} %constant_dynamic-slice_fusion), channel_id=1, source_target_pairs={{0,4},{4,8},{8,12},{12,0},{1,5},{5,9},{9,13},{13,1},{2,6},{6,10},{... | collective-permute-start | bytes 393224 | tf_op jit(solution)/shard_map/ppermute | solution.py:112
  4.1 2.6 %collective-permute-start.8 = (f32[8,4096]{1,0:T(8,128)S(1)}, f32[8,4096]{1,0:T(8,128)}, u32[]{:S(2)}, u32[]{:S(2)}) collective-permute-start(f32[8,4096]{1,0:T(8,128)S(1)} %constant_dynamic-slice_fusion), channel_id=1, source_target_pairs={{0,8},{4,12},{8,0},{12,4},{1,9},{5,13},{9,1},{13,5},{2,10},{6,14},... | collective-permute-start | bytes 393224 | tf_op jit(solution)/shard_map/ppermute | solution.py:112
  6.7 1.3 %collective-permute-start.10 = (f32[8,4096]{1,0:T(8,128)S(1)}, f32[8,4096]{1,0:T(8,128)}, u32[]{:S(2)}, u32[]{:S(2)}) collective-permute-start(f32[8,4096]{1,0:T(8,128)S(1)} %constant_dynamic-slice_fusion), channel_id=1, source_target_pairs={{0,12},{4,0},{8,4},{12,8},{1,13},{5,1},{9,5},{13,9},{2,14},{6,2},{... | collective-permute-start | bytes 393224 | tf_op jit(solution)/shard_map/ppermute | solution.py:112
  8.1 0.0 collective-permute-start.5
  8.1 1.5 %collective-permute-start.3 = (bf16[64,2048]{1,0:T(8,128)(2,1)}, bf16[64,2048]{1,0:T(8,128)(2,1)}, u32[]{:S(2)}, u32[]{:S(2)}) collective-permute-start(bf16[64,2048]{1,0:T(8,128)(2,1)} %refs_2_.3), channel_id=1, source_target_pairs={{2,0},{0,2},{3,1},{1,3},{6,4},{4,6},{7,5},{5,7},{10,8},{8,10},{11,... | collective-permute-start | bytes 786440 | tf_op jit(solution)/shard_map/ppermute | solution.py:134
  9.6 0.1 broadcast_in_dim.4
  9.7 1.0 %bitcast_dynamic-update-slice_fusion = f32[4,16,4096]{2,1,0:T(8,128)S(1)} fusion(f32[4,16,4096]{2,1,0:T(8,128)S(1)} %broadcast_in_dim.4, s32[]{:T(128)S(6)} %select_n.74, f32[16,4096]{1,0:T(8,128)} %param.13), kind=kLoop, calls=%fused_computation.6 | loop fusion | bytes 524292 | tf_op jit(solution)/shard_map/dynamic_update_slice | solution.py:110
  10.6 0.1 collective-permute-done.6
  10.7 0.2 collective-permute-start.7
  11.0 0.1 pad_add_fusion.refs_0_
  11.0 0.1 pad_add_fusion.1.refs_0_
  11.1 4.4 %collective-permute-done.8 = f32[8,4096]{1,0:T(8,128)} collective-permute-done((f32[8,4096]{1,0:T(8,128)S(1)}, f32[8,4096]{1,0:T(8,128)}, u32[]{:S(2)}, u32[]{:S(2)}) %collective-permute-start.8) | collective-permute-done | bytes 131104 | tf_op jit(solution)/shard_map/ppermute | solution.py:112
  15.5 0.0 collective-permute-start.2
  15.5 0.5 %collective-permute-start.9 = (f32[8,4096]{1,0:T(8,128)}, f32[8,4096]{1,0:T(8,128)S(1)}, u32[]{:S(2)}, u32[]{:S(2)}) collective-permute-start(f32[8,4096]{1,0:T(8,128)} %collective-permute-done.8), channel_id=1, source_target_pairs={{0,1},{1,0},{2,3},{3,2},{4,5},{5,4},{6,7},{7,6},{8,9},{9,8},{10,11... | collective-permute-start | bytes 393224 | tf_op jit(solution)/shard_map/ppermute | solution.py:113
  16.0 1.1 %fusion = f32[4,16,4096]{2,1,0:T(8,128)S(1)} fusion(f32[4,16,4096]{2,1,0:T(8,128)S(1)} %bitcast_dynamic-update-slice_fusion, s32[]{:T(128)S(6)} %select_n.79, f32[1,8,4096]{2,1,0:T(8,128)} %bitcast.6, f32[1,8,4096]{2,1,0:T(8,128)} %bitcast.5, pred[]{:T(512)S(6)} %eq.11), kind=kLoop, calls=%fused_computation.1 | loop fusion | flops 196608 | bytes 524293 | tf_op jit(solution)/shard_map/dynamic_update_slice | solution.py:119
  17.1 1.6 %collective-permute-start = (bf16[64,2048]{1,0:T(8,128)(2,1)}, bf16[64,2048]{1,0:T(8,128)(2,1)S(1)}, u32[]{:S(2)}, u32[]{:S(2)}) collective-permute-start(bf16[64,2048]{1,0:T(8,128)(2,1)} %refs_2_.2), channel_id=1, source_target_pairs={{2,0},{0,2},{3,1},{1,3},{6,4},{4,6},{7,5},{5,7},{10,8},{8,10},{11,... | collective-permute-start | bytes 786440 | tf_op jit(solution)/shard_map/ppermute | solution.py:134
  18.7 0.0 collective-permute-done.9
  18.7 0.0 collective-permute-start.11
  18.7 1.0 %fusion.1 = f32[4,16,4096]{2,1,0:T(8,128)S(1)} fusion(f32[4,16,4096]{2,1,0:T(8,128)S(1)} %fusion, s32[]{:T(128)S(6)} %select_n.82, f32[1,8,4096]{2,1,0:T(8,128)S(1)} %bitcast.16, f32[1,8,4096]{2,1,0:T(8,128)} %bitcast.7, pred[]{:T(512)S(6)} %eq.11), kind=kLoop, calls=%fused_computation.3 | loop fusion | flops 196608 | bytes 524293 | tf_op jit(solution)/shard_map/dynamic_update_slice | solution.py:119
  19.7 0.0 collective-permute-done.3.refs_2_
  19.7 0.6 %collective-permute-start.4 = (bf16[64,2048]{1,0:T(8,128)(2,1)}, bf16[64,2048]{1,0:T(8,128)(2,1)S(1)}, u32[]{:S(2)}, u32[]{:S(2)}) collective-permute-start(bf16[64,2048]{1,0:T(8,128)(2,1)} %collective-permute-done.3.refs_2_), channel_id=1, source_target_pairs={{0,1},{1,0},{2,3},{3,2},{4,5},{5,4},{6,7},{7,6},{8,9},{9,8},{10,11... | collective-permute-start | bytes 786440 | tf_op jit(solution)/shard_map/ppermute | solution.py:131
  20.3 5.3 %collective-permute-done.refs_2_ = bf16[64,2048]{1,0:T(8,128)(2,1)S(1)} collective-permute-done((bf16[64,2048]{1,0:T(8,128)(2,1)}, bf16[64,2048]{1,0:T(8,128)(2,1)S(1)}, u32[]{:S(2)}, u32[]{:S(2)}) %collective-permute-start) | collective-permute-done | bytes 262176 | tf_op jit(solution)/shard_map/ppermute | solution.py:134
  25.7 2.1 %shard_map.75.refs_4_ = f32[64,128]{1,0:T(8,128)S(1)} custom-call(s32[2]{0:T(128)S(1)} %pad_add_fusion.1.refs_0_, bf16[128,8192]{1,0:T(8,128)(2,1)S(1)} %copy-done, bf16[64,2048]{1,0:T(8,128)(2,1)S(1)} %copy-done.2, bf16[64,2048]{1,0:T(8,128)(2,1)} %collective-permute-done.5.refs_3_), custom_call_target="tpu_custom_call" | custom-call | flops 67108864 | bytes 1572864 | tf_op jit(solution)/shard_map/pallas_call | solution.py:48
  27.8 1.2 %shard_map.73.refs_4_ = f32[64,128]{1,0:T(8,128)S(1)} custom-call(s32[2]{0:T(128)S(1)} %pad_add_fusion.1.refs_0_, bf16[128,8192]{1,0:T(8,128)(2,1)S(1)} %copy-done.1, bf16[64,2048]{1,0:T(8,128)(2,1)S(1)} %copy-done.3, bf16[64,2048]{1,0:T(8,128)(2,1)S(1)} %collective-permute-done.2.refs_3_), custom_call_target="tpu_custom_call" | custom-call | flops 67108864 | bytes 1572864 | tf_op jit(solution)/shard_map/pallas_call | solution.py:48
  29.0 1.0 %fusion.2 = f32[4,16,4096]{2,1,0:T(8,128)S(1)} fusion(f32[4,16,4096]{2,1,0:T(8,128)S(1)} %fusion.1, s32[]{:T(128)S(6)} %select_n.85, f32[1,8,4096]{2,1,0:T(8,128)S(1)} %bitcast.15, f32[1,8,4096]{2,1,0:T(8,128)} %bitcast.9, pred[]{:T(512)S(6)} %eq.11), kind=kLoop, calls=%fused_computation.5 | loop fusion | flops 196608 | bytes 524293 | tf_op jit(solution)/shard_map/dynamic_update_slice | solution.py:119
  30.1 0.0 copy-start.4
  30.1 0.0 copy-start.5
  30.1 2.1 %shard_map.76.out_ref = f32[64,128]{1,0:T(8,128)S(1)} custom-call(s32[2]{0:T(128)S(1)} %pad_add_fusion.refs_0_, bf16[128,8192]{1,0:T(8,128)(2,1)S(1)} %copy-done, bf16[64,2048]{1,0:T(8,128)(2,1)} %collective-permute-done.3.refs_2_, bf16[64,2048]{1,0:T(8,128)(2,1)S(1)} %collective-permute-done.4.refs_3_, f32[64,128]{1,0:T(8,128)S(1)} %shard_map.75.refs_4_), custom_call_target="tpu_custom_call" | custom-call | flops 67108864 | bytes 1572864 | tf_op jit(solution)/shard_map/pallas_call | solution.py:48
  32.2 0.0 collective-permute-done.1.refs_3_
  32.2 1.2 %shard_map.74.in_ref = f32[64,128]{1,0:T(8,128)S(1)} custom-call(s32[2]{0:T(128)S(1)} %pad_add_fusion.refs_0_, bf16[128,8192]{1,0:T(8,128)(2,1)S(1)} %copy-done.1, bf16[64,2048]{1,0:T(8,128)(2,1)S(1)} %collective-permute-done.refs_2_, bf16[64,2048]{1,0:T(8,128)(2,1)S(1)} %collective-permute-done.1.refs_3_, f32[64,128]{1,0:T(8,128)S(1)} %shard_map.73.refs_4_), custom_call_target="tpu_custom_call" | custom-call | flops 67108864 | bytes 1572864 | tf_op jit(solution)/shard_map/pallas_call | solution.py:48
  33.5 2.3 %shard_map.77 = f32[8,64]{1,0:T(8,128)} custom-call(f32[64,128]{1,0:T(8,128)S(1)} %shard_map.74.in_ref, f32[64,128]{1,0:T(8,128)S(1)} %shard_map.76.out_ref, s32[1,128]{1,0:T(1,128)S(1)} %copy-done.4, s32[1,128]{1,0:T(1,128)S(1)} %copy-done.5, f32[64,4096]{1,0:T(8,128)S(1)} %bitcast.14), custom_call_target="tpu_custom_call" | custom-call | flops 75497472 | bytes 1048576 | tf_op jit(solution)/shard_map/pallas_call | solution.py:88
  (17 shorter events, 0.0 us)
Async XLA Ops:
  0.0 25.6 %copy-start.2 = (bf16[64,2048]{1,0:T(8,128)(2,1)S(1)}, bf16[64,2048]{1,0:T(8,128)(2,1)}, u32[]{:S(2)}) copy-start(bf16[64,2048]{1,0:T(8,128)(2,1)} %refs_2_.3) | copy-start | bytes 786436
  0.0 25.6 %copy-start = (bf16[128,8192]{1,0:T(8,128)(2,1)S(1)}, bf16[128,8192]{1,0:T(8,128)(2,1)}, u32[]{:S(2)}) copy-start(bf16[128,8192]{1,0:T(8,128)(2,1)} %refs_1_.7) | copy-start | bytes 6291460
  1.1 9.6 %collective-permute-start.6 = (f32[8,4096]{1,0:T(8,128)S(1)}, f32[8,4096]{1,0:T(8,128)}, u32[]{:S(2)}, u32[]{:S(2)}) collective-permute-start(f32[8,4096]{1,0:T(8,128)S(1)} %constant_dynamic-slice_fusion), channel_id=1, source_target_pairs={{0,4},{4,8},{8,12},{12,0},{1,5},{5,9},{9,13},{13,1},{2,6},{6,10},{... | collective-permute-start | bytes 393224 | tf_op jit(solution)/shard_map/ppermute | solution.py:112
  4.1 11.3 %collective-permute-start.8 = (f32[8,4096]{1,0:T(8,128)S(1)}, f32[8,4096]{1,0:T(8,128)}, u32[]{:S(2)}, u32[]{:S(2)}) collective-permute-start(f32[8,4096]{1,0:T(8,128)S(1)} %constant_dynamic-slice_fusion), channel_id=1, source_target_pairs={{0,8},{4,12},{8,0},{12,4},{1,9},{5,13},{9,1},{13,5},{2,10},{6,14},... | collective-permute-start | bytes 393224 | tf_op jit(solution)/shard_map/ppermute | solution.py:112
  6.7 10.4 %collective-permute-start.10 = (f32[8,4096]{1,0:T(8,128)S(1)}, f32[8,4096]{1,0:T(8,128)}, u32[]{:S(2)}, u32[]{:S(2)}) collective-permute-start(f32[8,4096]{1,0:T(8,128)S(1)} %constant_dynamic-slice_fusion), channel_id=1, source_target_pairs={{0,12},{4,0},{8,4},{12,8},{1,13},{5,1},{9,5},{13,9},{2,14},{6,2},{... | collective-permute-start | bytes 393224 | tf_op jit(solution)/shard_map/ppermute | solution.py:112
  8.1 17.5 %collective-permute-start.5 = (bf16[64,2048]{1,0:T(8,128)(2,1)}, bf16[64,2048]{1,0:T(8,128)(2,1)}, u32[]{:S(2)}, u32[]{:S(2)}) collective-permute-start(bf16[64,2048]{1,0:T(8,128)(2,1)} %refs_2_.3), channel_id=1, source_target_pairs={{0,1},{1,0},{2,3},{3,2},{4,5},{5,4},{6,7},{7,6},{8,9},{9,8},{10,11... | collective-permute-start | bytes 786440 | tf_op jit(solution)/shard_map/ppermute | solution.py:131
  8.1 11.6 %collective-permute-start.3 = (bf16[64,2048]{1,0:T(8,128)(2,1)}, bf16[64,2048]{1,0:T(8,128)(2,1)}, u32[]{:S(2)}, u32[]{:S(2)}) collective-permute-start(bf16[64,2048]{1,0:T(8,128)(2,1)} %refs_2_.3), channel_id=1, source_target_pairs={{2,0},{0,2},{3,1},{1,3},{6,4},{4,6},{7,5},{5,7},{10,8},{8,10},{11,... | collective-permute-start | bytes 786440 | tf_op jit(solution)/shard_map/ppermute | solution.py:134
  10.7 4.8 %collective-permute-start.7 = (f32[8,4096]{1,0:T(8,128)}, f32[8,4096]{1,0:T(8,128)}, u32[]{:S(2)}, u32[]{:S(2)}) collective-permute-start(f32[8,4096]{1,0:T(8,128)} %collective-permute-done.6), channel_id=1, source_target_pairs={{0,1},{1,0},{2,3},{3,2},{4,5},{5,4},{6,7},{7,6},{8,9},{9,8},{10,11... | collective-permute-start | bytes 393224 | tf_op jit(solution)/shard_map/ppermute | solution.py:113
  11.0 16.8 %copy-start.1 = (bf16[128,8192]{1,0:T(8,128)(2,1)S(1)}, bf16[128,8192]{1,0:T(8,128)(2,1)}, u32[]{:S(2)}) copy-start(bf16[128,8192]{1,0:T(8,128)(2,1)} %refs_1_.5) | copy-start | bytes 6291460
  11.0 16.8 %copy-start.3 = (bf16[64,2048]{1,0:T(8,128)(2,1)S(1)}, bf16[64,2048]{1,0:T(8,128)(2,1)}, u32[]{:S(2)}) copy-start(bf16[64,2048]{1,0:T(8,128)(2,1)} %refs_2_.2) | copy-start | bytes 786436
  15.5 12.3 %collective-permute-start.2 = (bf16[64,2048]{1,0:T(8,128)(2,1)}, bf16[64,2048]{1,0:T(8,128)(2,1)S(1)}, u32[]{:S(2)}, u32[]{:S(2)}) collective-permute-start(bf16[64,2048]{1,0:T(8,128)(2,1)} %refs_2_.2), channel_id=1, source_target_pairs={{0,1},{1,0},{2,3},{3,2},{4,5},{5,4},{6,7},{7,6},{8,9},{9,8},{10,11... | collective-permute-start | bytes 786440 | tf_op jit(solution)/shard_map/ppermute | solution.py:131
  15.5 3.2 %collective-permute-start.9 = (f32[8,4096]{1,0:T(8,128)}, f32[8,4096]{1,0:T(8,128)S(1)}, u32[]{:S(2)}, u32[]{:S(2)}) collective-permute-start(f32[8,4096]{1,0:T(8,128)} %collective-permute-done.8), channel_id=1, source_target_pairs={{0,1},{1,0},{2,3},{3,2},{4,5},{5,4},{6,7},{7,6},{8,9},{9,8},{10,11... | collective-permute-start | bytes 393224 | tf_op jit(solution)/shard_map/ppermute | solution.py:113
  17.1 8.5 %collective-permute-start = (bf16[64,2048]{1,0:T(8,128)(2,1)}, bf16[64,2048]{1,0:T(8,128)(2,1)S(1)}, u32[]{:S(2)}, u32[]{:S(2)}) collective-permute-start(bf16[64,2048]{1,0:T(8,128)(2,1)} %refs_2_.2), channel_id=1, source_target_pairs={{2,0},{0,2},{3,1},{1,3},{6,4},{4,6},{7,5},{5,7},{10,8},{8,10},{11,... | collective-permute-start | bytes 786440 | tf_op jit(solution)/shard_map/ppermute | solution.py:134
  18.7 10.3 %collective-permute-start.11 = (f32[8,4096]{1,0:T(8,128)}, f32[8,4096]{1,0:T(8,128)S(1)}, u32[]{:S(2)}, u32[]{:S(2)}) collective-permute-start(f32[8,4096]{1,0:T(8,128)} %collective-permute-done.10), channel_id=1, source_target_pairs={{0,1},{1,0},{2,3},{3,2},{4,5},{5,4},{6,7},{7,6},{8,9},{9,8},{10,11... | collective-permute-start | bytes 393224 | tf_op jit(solution)/shard_map/ppermute | solution.py:113
  19.7 10.4 %collective-permute-start.4 = (bf16[64,2048]{1,0:T(8,128)(2,1)}, bf16[64,2048]{1,0:T(8,128)(2,1)S(1)}, u32[]{:S(2)}, u32[]{:S(2)}) collective-permute-start(bf16[64,2048]{1,0:T(8,128)(2,1)} %collective-permute-done.3.refs_2_), channel_id=1, source_target_pairs={{0,1},{1,0},{2,3},{3,2},{4,5},{5,4},{6,7},{7,6},{8,9},{9,8},{10,11... | collective-permute-start | bytes 786440 | tf_op jit(solution)/shard_map/ppermute | solution.py:131
  25.6 6.6 %collective-permute-start.1 = (bf16[64,2048]{1,0:T(8,128)(2,1)S(1)}, bf16[64,2048]{1,0:T(8,128)(2,1)S(1)}, u32[]{:S(2)}, u32[]{:S(2)}) collective-permute-start(bf16[64,2048]{1,0:T(8,128)(2,1)S(1)} %collective-permute-done.refs_2_), channel_id=1, source_target_pairs={{0,1},{1,0},{2,3},{3,2},{4,5},{5,4},{6,7},{7,6},{8,9},{9,8},{10,11... | collective-permute-start | bytes 786440 | tf_op jit(solution)/shard_map/ppermute | solution.py:131
  30.1 3.4 %copy-start.4 = (s32[1,128]{1,0:T(1,128)S(1)}, s32[1,128]{1,0:T(1,128)}, u32[]{:S(2)}) copy-start(s32[1,128]{1,0:T(1,128)} %seg_ref.1) | copy-start | bytes 1540
  30.1 3.4 %copy-start.5 = (s32[1,128]{1,0:T(1,128)S(1)}, s32[1,128]{1,0:T(1,128)}, u32[]{:S(2)}) copy-start(s32[1,128]{1,0:T(1,128)} %mask_ref.1) | copy-start | bytes 1540

commit v2 on v0

v2 whole, which is shorter than its diff:
```python
import jax
import jax.numpy as jnp
from jax import lax
from jax.experimental import pallas as pl
from jax.experimental.pallas import tpu as pltpu
from jax.sharding import PartitionSpec as P

TRAJ_DEV = 8
NT = (((1,), (1,)), ((), ()))
ANY = pl.BlockSpec(memory_space=pl.ANY)
VMEM = pl.BlockSpec(memory_space=pltpu.VMEM)
SMEM = pl.BlockSpec(memory_space=pltpu.SMEM)
SMALL = pltpu.CompilerParams(vmem_limit_bytes=8 << 20)
PARAMS = pltpu.CompilerParams(vmem_limit_bytes=52 << 20)


def dot_nt(a, b):
    return lax.dot_general(a, b, NT, preferred_element_type=jnp.float32)


def halves(a):
    high = a.astype(jnp.bfloat16)
    return high, (a - high.astype(jnp.float32)).astype(jnp.bfloat16)


class Chunks:
    def __init__(self, toks_hbm, owner_ref, projs_hbm, toks, projs, sems, first):
        width = projs.shape[2]
        self.toks, self.projs, self.first, self.copies = toks, projs, first, []
        for i, proj in enumerate(projs_hbm):
            k = first + i
            columns = pl.ds(pl.multiple_of(owner_ref[i] * width, 128), width)
            pair = (
                pltpu.make_async_copy(proj, projs.at[k], sems.at[0, k]),
                pltpu.make_async_copy(toks_hbm.at[:, columns], toks.at[k], sems.at[1, k]),
            )
            for copy in pair:
                copy.start()
            self.copies.append(pair)

    def total(self, base):
        for i, pair in enumerate(self.copies):
            for copy in pair:
                copy.wait()
            part = dot_nt(self.toks[self.first + i], self.projs[self.first + i])
            base = part if base is None else base + part
        return base


def chunk_scratch(n, toks, projs):
    rank, width = projs[0].shape
    return [
        pltpu.VMEM((n, toks.shape[0], width), toks.dtype),
        pltpu.VMEM((n, rank, width), projs[0].dtype),
        pltpu.SemaphoreType.DMA((2, n)),
    ]


def project(acts, grads, in_owners, in_projs, out_owners, out_projs, bases):
    rank = in_projs[0].shape[0]
    count = acts.shape[0]
    n, m = len(in_projs), len(out_projs)

    def kernel(in_owner_ref, out_owner_ref, act, grad, *refs):
        proj_hbm, base_refs, refs = refs[: n + m], refs[n + m : -5], refs[-5:]
        in_ref, out_ref, *scratch = refs
        ins = Chunks(act, in_owner_ref, proj_hbm[:n], *scratch, 0)
        outs = Chunks(grad, out_owner_ref, proj_hbm[n:], *scratch, n)
        in_ref[...] = ins.total(base_refs[0][...] if bases else None)
        out_ref[...] = outs.total(base_refs[1][...] if bases else None)

    sums = jax.ShapeDtypeStruct((count, rank), jnp.float32)
    return pl.pallas_call(
        kernel,
        out_shape=(sums, sums),
        in_specs=[SMEM] * 2 + [ANY] * (2 + n + m) + [VMEM] * len(bases),
        out_specs=(VMEM, VMEM),
        scratch_shapes=chunk_scratch(n + m, acts, in_projs),
        compiler_params=PARAMS,
        cost_estimate=cost(),
    )(in_owners, out_owners, acts, grads, *in_projs, *out_projs, *bases)


def partial_scores(queries, f_stack):
    q_high, q_low = halves(queries)
    both = dot_nt(f_stack, q_high)
    return both[:TRAJ_DEV] + both[TRAJ_DEV:] + dot_nt(f_stack, q_low)[:TRAJ_DEV]


def spread_blocks(scores, places, slots):
    rows = scores.shape[1] // len(places)
    block = lax.broadcasted_iota(jnp.int32, (TRAJ_DEV, rows * slots), 1) // rows
    ordered = jnp.zeros((TRAJ_DEV, rows * slots), jnp.float32)
    for s, place in enumerate(places):
        piece = scores[:, s * rows : (s + 1) * rows]
        ordered = jnp.where(block == place, jnp.concatenate([piece] * slots, axis=1), ordered)
    return ordered


def gradients(
    acts, grads, in_owners, in_projs, out_owners, out_projs, bases, segments, loss_mask, places, pieces, slots
):
    count, rank = bases[0].shape
    rows, flat_width = pieces[0].shape
    n, m, k = len(in_projs), len(out_projs), len(pieces)

    def kernel(in_owner_ref, out_owner_ref, place_ref, act, grad, *refs):
        proj_hbm, piece_hbm, refs = refs[: n + m], refs[n + m : n + m + k], refs[n + m + k :]
        in_base, out_base, seg_ref, mask_ref, stack_ref, score_ref = refs[:6]
        *scratch, blocks, block_sems = refs[6:]
        ins = Chunks(act, in_owner_ref, proj_hbm[:n], *scratch, 0)
        outs = Chunks(grad, out_owner_ref, proj_hbm[n:], *scratch, n)
        copies = [
            pltpu.make_async_copy(piece, blocks.at[pl.ds(i * rows, rows)], block_sems.at[i])
            for i, piece in enumerate(piece_hbm)
        ]
        for copy in copies:
            copy.start()
        own = seg_ref[...] == lax.broadcasted_iota(jnp.int32, (TRAJ_DEV, count), 0)
        masked = jnp.where(own, mask_ref[...].astype(jnp.float32), 0.0)
        counts = jnp.sum(masked, axis=1, keepdims=True)
        weight = masked * (1.0 / jnp.maximum(counts, 1.0))
        in_t = ins.total(in_base[...]).T
        t_high, t_low = halves(jnp.concatenate([in_t, in_t], axis=0))
        out_t = outs.total(out_base[...]).T
        left = (out_t[:, None, :] * weight[None]).reshape(rank * TRAJ_DEV, count)
        l_high, l_low = halves(left)
        outer = dot_nt(
            jnp.concatenate([l_high, l_low], axis=1), jnp.concatenate([t_high, t_high], axis=1)
        ) + dot_nt(l_high, t_low)
        outer = outer.reshape(rank // 2, 2, TRAJ_DEV, 2 * rank)
        low = lax.broadcasted_iota(jnp.int32, (TRAJ_DEV, 2 * rank), 1) < rank
        flat = jnp.concatenate(
            [jnp.where(low, outer[p, 0], outer[p, 1]) for p in range(rank // 2)], axis=1
        )
        f_stack = jnp.concatenate(halves(flat), axis=0)
        for copy in copies:
            copy.wait()
        scores = partial_scores(blocks[...], f_stack)
        stack_ref[...] = f_stack
        score_ref[...] = spread_blocks(scores, [place_ref[s] for s in range(k)], slots)

    return pl.pallas_call(
        kernel,
        out_shape=(
            jax.ShapeDtypeStruct((2 * TRAJ_DEV, flat_width), jnp.bfloat16),
            jax.ShapeDtypeStruct((TRAJ_DEV, rows * slots), jnp.float32),
        ),
        in_specs=[SMEM] * 3 + [ANY] * (2 + n + m + k) + [VMEM] * 4,
        out_specs=(VMEM, VMEM),
        scratch_shapes=chunk_scratch(n + m, acts, in_projs)
        + [pltpu.VMEM((k * rows, flat_width), jnp.float32), pltpu.SemaphoreType.DMA((k,))],
        compiler_params=PARAMS,
        cost_estimate=cost(),
    )(
        in_owners,
        out_owners,
        places,
        acts,
        grads,
        *in_projs,
        *out_projs,
        *pieces,
        *bases,
        segments,
        loss_mask,
    )


def last_block(places, scores, f_stack, here, there):
    slots = scores.shape[1] // here.shape[0]
    at = places.shape[0] - 2

    def kernel(place_ref, base_ref, stack_ref, here_ref, there_ref, score_ref):
        block = jnp.where(place_ref[at + 1] == 0, here_ref[...], there_ref[...])
        scores = partial_scores(block, stack_ref[...])
        score_ref[...] = base_ref[...] + spread_blocks(scores, [place_ref[at]], slots)

    return pl.pallas_call(
        kernel,
        out_shape=jax.ShapeDtypeStruct(scores.shape, jnp.float32),
        in_specs=[SMEM] + [VMEM] * 4,
        out_specs=VMEM,
        compiler_params=SMALL,
        cost_estimate=cost(),
    )(places, scores, f_stack, here, there)


def cost():
    return pl.CostEstimate(flops=1, bytes_accessed=1, transcendentals=0)


def fetch_queries(queries, sizes):
    n = sizes["traj"]
    if n != 4:
        return [lax.all_gather(queries, "traj", axis=0, tiled=True)]
    line = range(n)
    beside = lax.ppermute(
        queries,
        ("traj", "sub"),
        [(2 * ((z + 1) % n), 2 * z) for z in line]
        + [(2 * ((z + n - 1) % n) + 1, 2 * z + 1) for z in line],
    )
    across = lax.ppermute(queries, ("traj", "sub"), [(2 * ((z + 2) % n), 2 * z) for z in line])
    return [beside, across]


def query_places(at, core):
    step = jnp.where(core == 0, 1, 3)
    places = jnp.stack([at, (at + step) % 4, (at + 4 - step) % 4, (at + 2) % 4, core])
    return places.astype(jnp.int32)


def body(sizes, activations, out_grads, segments, loss_mask, proj_in, proj_out, queries):
    chips = sizes["fsdp"]
    x, core = lax.axis_index("fsdp"), lax.axis_index("sub")

    def to_core(a):
        return lax.ppermute(a, "sub", [(0, 1), (1, 0)])

    def from_chip(a, d):
        return lax.ppermute(a, "fsdp", [((i + d) % chips, i) for i in range(chips)])

    def after(arrays, *waited):
        return lax.optimization_barrier((arrays, *waited))

    def numbers(*owners):
        return jnp.stack(owners).astype(jnp.int32)

    far_in = [from_chip(proj_in, d) for d in range(1, chips)]
    far_out = [from_chip(proj_out, d) for d in range(1, chips)]
    fetched = fetch_queries(queries, sizes)
    own, other = 2 * x + core, 2 * x + 1 - core
    far_own = [2 * ((x + d) % chips) + core for d in range(1, chips)]
    far_other = [2 * ((x + d) % chips) + 1 - core for d in range(1, chips)]

    places = query_places(lax.axis_index("traj"), core)
    sums = project(
        activations,
        out_grads,
        numbers(own, other),
        [proj_in, to_core(proj_in)],
        numbers(own),
        [proj_out],
        [],
    )
    (far_in, far_out, late_out), sums = after((far_in, far_out, proj_out), sums)
    others_in = [to_core(a) for a in far_in]
    others_out = [to_core(a) for a in far_out] + [to_core(late_out)]
    on_line = len(fetched) > 1
    if on_line:
        beside, across = fetched
        pieces = [queries, beside, to_core(beside)]
    else:
        pieces, places = fetched, jnp.zeros((1,), jnp.int32)
    sums = project(
        activations, out_grads, numbers(*far_own), far_in, numbers(*far_own), far_out, sums
    )
    if on_line:
        across, sums = after(across, sums)
        across_other = to_core(across)
    f_stack, scores = gradients(
        activations,
        out_grads,
        numbers(*far_other),
        others_in,
        numbers(*far_other, other),
        others_out,
        sums,
        segments,
        loss_mask,
        places,
        pieces,
        4 if on_line else 1,
    )
    if on_line:
        scores = last_block(places, scores, f_stack, across, across_other)
    return scores.T


def solution(mesh):
    placed = (
        P(("groups", "traj", "fsdp", "sub"), None),
        P(("groups", "traj", "fsdp", "sub"), None),
        P(("groups", "traj", "fsdp", "sub"), None),
        P(("groups", "traj", "fsdp", "sub"), None),
        P(None, ("fsdp", "sub")),
        P(None, ("fsdp", "sub")),
        P(("groups", "traj"), None),
    )
    sizes = dict(mesh.shape)

    def program(*arrays):
        return body(sizes, *arrays)

    return jax.shard_map(
        program,
        mesh=mesh,
        in_specs=placed,
        out_specs=P("groups", ("traj", "fsdp", "sub")),
        check_vma=False,
    )
```

time: 85.7 us -> 25 us (0.29)
  waiting for transfers between devices: 60.9 us -> 3.76 us
  between operations: 13.1 us -> 0.12 us
  matrix products: 11.1 us -> 0 us
  starting transfers between devices: 0.08 us -> 10 us
  Pallas kernels: 0 us -> 9.6 us
  local copies, waits for them, and re-layouts: 0.01 us -> 1.05 us
    all_gather x3 -> x0, waiting for transfers between devices: 58.8 us -> none  [the longest x1 24.7 us: body(): lax.all_gather(queries, 'traj', axis=0, tiled=True)]
    dot_general x6 -> x0, matrix products: 11.1 us -> none  [the longest x1 2.74 us: body(): lax.dot_general(lax.all_gather(queries, 'traj', axis=0, tiled=True), trai...]
    ppermute x0 -> x10, starting transfers between devices: none -> 10 us  [the longest x1 4.07 us: fetch_queries(): lax.ppermute(queries, ('traj', 'sub'), [(2 * ((z + 1) % n), 2 * z) for z...]
    pallas_call x0 -> x4, Pallas kernels: none -> 9.6 us  [the longest x2 4.48 us: project(): pl.pallas_call(kernel, out_shape=(sums, sums), in_specs=[SMEM] * 2 + [ANY...]
    ppermute x0 -> x10, waiting for transfers between devices: none -> 3.76 us  [the longest x2 2.92 us: from_chip(): return lax.ppermute(a, 'fsdp', [((i + d) % chips, i) for i in range(chips)])]
    unnamed x3 -> x0, waiting for transfers between devices: 2.09 us -> none
    unnamed x4 -> x8, local copies, waits for them, and re-layouts: 0.01 us -> 0.96 us
  transfers between devices with their start and end apart: 3 -> 10, of which waited for: 3 -> 2; matrix products, arithmetic and copies ran while one was open for 10% -> 1% of each run, Pallas kernels for 0% -> 33%
where the time goes in v2:
time: 25 us; the launch traced here: 24.7 us
  starting transfers between devices  10 us (40%)
  Pallas kernels  9.6 us (38%)
  waiting for transfers between devices  3.76 us (15%)
  local copies, waits for them, and re-layouts  1.05 us (4%)
    pallas_call x2, Pallas kernels, project(): pl.pallas_call(kernel, out_shape=(sums, sums), in_specs=[SMEM] * 2 + [ANY...  4.48 us
    ppermute x1, starting transfers between devices, fetch_queries(): lax.ppermute(queries, ('traj', 'sub'), [(2 * ((z + 1) % n), 2 * z) for z...  4.07 us
    pallas_call x1, Pallas kernels, gradients(): pl.pallas_call(kernel, out_shape=(jax.ShapeDtypeStruct((2 * TRAJ_DEV, fla...  3.67 us
    ppermute x2, waiting for transfers between devices, from_chip(): return lax.ppermute(a, 'fsdp', [((i + d) % chips, i) for i in range(chips)])  2.92 us
    ppermute x2, starting transfers between devices, from_chip(): return lax.ppermute(a, 'fsdp', [((i + d) % chips, i) for i in range(chips)])  2.56 us
    ppermute x1, starting transfers between devices, fetch_queries(): lax.ppermute(queries, ('traj', 'sub'), [(2 * ((z + 2) % n), 2 * z) for z...  1.91 us
    ppermute x6, starting transfers between devices, to_core(): return lax.ppermute(a, 'sub', [(0, 1), (1, 0)])  1.48 us
    pallas_call x1, Pallas kernels, last_block(): pl.pallas_call(kernel, out_shape=jax.ShapeDtypeStruct(scores.shape, jnp.f...  1.45 us
  transfers between devices with their start and end apart: 10, of which 2 were waited for; matrix products, arithmetic and copies ran while one was open for 1% of the time, Pallas kernels for 33%

profile of v2, /device:TPU:0, one launch (start us, length us, event | category | flops | bytes accessed | tf_op | source)
XLA Modules:
  0.0 24.7 jit_solution(981248480657103746)
XLA Ops:
  0.0 0.5 %collective-permute-start.2 = (bf16[64,2048]{1,0:T(8,128)(2,1)}, bf16[64,2048]{1,0:T(8,128)(2,1)S(1)}, u32[]{:S(2)}, u32[]{:S(2)}) collective-permute-start(bf16[64,2048]{1,0:T(8,128)(2,1)} %refs_0_.1), channel_id=1, source_target_pairs={{0,1},{1,0},{2,3},{3,2},{4,5},{5,4},{6,7},{7,6},{8,9},{9,8},{10,11... | collective-permute-start | bytes 786440 | tf_op jit(solution)/shard_map/ppermute | solution.py:219
  0.5 2.5 %collective-permute-start = (bf16[64,2048]{1,0:T(8,128)(2,1)}, bf16[64,2048]{1,0:T(8,128)(2,1)S(1)}, u32[]{:S(2)}, u32[]{:S(2)}) collective-permute-start(bf16[64,2048]{1,0:T(8,128)(2,1)} %refs_0_.1), channel_id=1, source_target_pairs={{2,0},{0,2},{3,1},{1,3},{6,4},{4,6},{7,5},{5,7},{10,8},{8,10},{11,... | collective-permute-start | bytes 786440 | tf_op jit(solution)/shard_map/ppermute | solution.py:222
  2.9 0.1 collective-permute-start.1
  3.0 4.1 %collective-permute-start.6 = (f32[16,4096]{1,0:T(8,128)}, f32[16,4096]{1,0:T(8,128)S(1)}, u32[]{:S(2)}, u32[]{:S(2)}) collective-permute-start(f32[16,4096]{1,0:T(8,128)} %refs_3_.1), channel_id=1, source_target_pairs={{4,0},{8,4},{12,8},{0,12},{13,1},{1,5},{5,9},{9,13},{6,2},{10,6},{... | collective-permute-start | bytes 786440 | tf_op jit(solution)/shard_map/ppermute | solution.py:198
  7.1 1.9 %collective-permute-start.8 = (f32[16,4096]{1,0:T(8,128)}, f32[16,4096]{1,0:T(8,128)S(1)}, u32[]{:S(2)}, u32[]{:S(2)}) collective-permute-start(f32[16,4096]{1,0:T(8,128)} %refs_3_.1), channel_id=1, source_target_pairs={{8,0},{12,4},{0,8},{4,12},{10,2},{14,6},{2,10},{6,14},{24,16},{28,... | collective-permute-start | bytes 786440 | tf_op jit(solution)/shard_map/ppermute | solution.py:204
  9.0 0.1 pad_add_fusion.1.in_owner_ref
  9.1 0.0 collective-permute-done.2.refs_1_
  9.1 0.0 copy-start.1
  9.1 0.9 %copy-done.1 = bf16[64,2048]{1,0:T(8,128)(2,1)S(1)} copy-done((bf16[64,2048]{1,0:T(8,128)(2,1)S(1)}, bf16[64,2048]{1,0:T(8,128)(2,1)}, u32[]{:S(2)}) %copy-start.1) | copy-done | bytes 262168
  10.0 2.8 %shard_map.73 = (f32[128,64]{1,0:T(8,128)S(1)}, f32[128,64]{1,0:T(8,128)S(1)}) custom-call(s32[2]{0:T(128)S(1)} %pad_add_fusion.1.in_owner_ref, s32[1]{0:T(128)} %bitcast.7.out_owner_ref, bf16[128,8192]{1,0:T(8,128)(2,1)} %act.5, bf16[128,8192]{1,0:T(8,128)(2,1)} %grad.5, bf16[64,2048]{1,0:T(8,128)(2,1)S(1)} %copy-done.1, ...), custom_call_target="tpu_custom_call" | custom-call | flops 1 | bytes 1 | tf_op jit(solution)/shard_map/pallas_call | solution.py:73
  12.8 0.0 collective-permute-done.refs_0_
  12.8 2.9 %collective-permute-done.1.refs_1_ = bf16[64,2048]{1,0:T(8,128)(2,1)S(1)} collective-permute-done((bf16[64,2048]{1,0:T(8,128)(2,1)}, bf16[64,2048]{1,0:T(8,128)(2,1)S(1)}, u32[]{:S(2)}, u32[]{:S(2)}) %collective-permute-start.1) | collective-permute-done | bytes 262176 | tf_op jit(solution)/shard_map/ppermute | solution.py:222
  15.7 0.0 collective-permute-start.5
  15.7 0.5 %collective-permute-start.3 = (bf16[64,2048]{1,0:T(8,128)(2,1)S(1)}, bf16[64,2048]{1,0:T(8,128)(2,1)S(1)}, u32[]{:S(2)}, u32[]{:S(2)}) collective-permute-start(bf16[64,2048]{1,0:T(8,128)(2,1)S(1)} %collective-permute-done.refs_0_), channel_id=1, source_target_pairs={{0,1},{1,0},{2,3},{3,2},{4,5},{5,4},{6,7},{7,6},{8,9},{9,8},{10,11... | collective-permute-start | bytes 786440 | tf_op jit(solution)/shard_map/ppermute | solution.py:219
  16.3 0.0 collective-permute-start.4
  16.3 0.0 collective-permute-done.6.refs_4_
  16.3 0.5 %collective-permute-start.7 = (f32[16,4096]{1,0:T(8,128)S(1)}, f32[16,4096]{1,0:T(8,128)S(1)}, u32[]{:S(2)}, u32[]{:S(2)}) collective-permute-start(f32[16,4096]{1,0:T(8,128)S(1)} %collective-permute-done.6.refs_4_), channel_id=1, source_target_pairs={{0,1},{1,0},{2,3},{3,2},{4,5},{5,4},{6,7},{7,6},{8,9},{9,8},{10,11... | collective-permute-start | bytes 786440 | tf_op jit(solution)/shard_map/ppermute | solution.py:219
  16.8 1.7 %shard_map.74 = (f32[128,64]{1,0:T(8,128)S(1)}, f32[128,64]{1,0:T(8,128)S(1)}) custom-call(s32[1]{0:T(128)} %bitcast.8.in_owner_ref.out_owner_ref, s32[1]{0:T(128)} %bitcast.8.in_owner_ref.out_owner_ref, bf16[128,8192]{1,0:T(8,128)(2,1)} %act.5, bf16[128,8192]{1,0:T(8,128)(2,1)} %grad.5, bf16[64,2048]{1,0:T(8,128)(2,1)S(1)} %collective-permute-done.refs_0_, ...), custom_call_target="tpu_custom_call" | custom-call | flops 1 | bytes 1 | tf_op jit(solution)/shard_map/pallas_call | solution.py:73
  18.5 0.8 %collective-permute-done.8.here_ref = f32[16,4096]{1,0:T(8,128)S(1)} collective-permute-done((f32[16,4096]{1,0:T(8,128)}, f32[16,4096]{1,0:T(8,128)S(1)}, u32[]{:S(2)}, u32[]{:S(2)}) %collective-permute-start.8) | collective-permute-done | bytes 262176 | tf_op jit(solution)/shard_map/ppermute | solution.py:204
  19.3 0.0 collective-permute-start.9
  19.3 0.1 stack.45.place_ref
  19.4 0.1 pad_add_fusion.out_owner_ref
  19.5 0.0 collective-permute-done.5.refs_2_
  19.5 0.0 collective-permute-done.3.refs_0_
  19.5 0.0 collective-permute-done.4.refs_1_
  19.5 0.0 collective-permute-done.7.refs_5_
  19.5 0.0 copy-done
  19.5 0.0 copy-done.2
  19.5 0.0 copy-done.3
  19.5 3.7 %shard_map.75 = (bf16[16,4096]{1,0:T(8,128)(2,1)S(1)}, f32[8,64]{1,0:T(8,128)S(1)}) custom-call(s32[1]{0:T(128)} %bitcast.5.in_owner_ref, s32[2]{0:T(128)S(1)} %pad_add_fusion.out_owner_ref, s32[5]{0:T(128)S(1)} %stack.45.place_ref, bf16[128,8192]{1,0:T(8,128)(2,1)} %act.5, bf16[128,8192]{1,0:T(8,128)(2,1)} %grad.5, ...), custom_call_target="tpu_custom_call" | custom-call | flops 1 | bytes 1 | tf_op jit(solution)/shard_map/pallas_call | solution.py:143
  23.2 0.0 collective-permute-done.9.there_ref
  23.2 1.4 %shard_map.76 = f32[8,64]{1,0:T(8,128)} custom-call(s32[5]{0:T(128)S(1)} %stack.45.place_ref, f32[8,64]{1,0:T(8,128)S(1)} %get-tuple-element.30.base_ref, bf16[16,4096]{1,0:T(8,128)(2,1)S(1)} %get-tuple-element.31.stack_ref, f32[16,4096]{1,0:T(8,128)S(1)} %collective-permute-done.8.here_ref, f32[16,4096]{1,0:T(8,128)S(1)} %collective-permute-done.9.there_ref), custom_call_target="tpu_custom_call" | custom-call | flops 1 | bytes 1 | tf_op jit(solution)/shard_map/pallas_call | solution.py:179
  (3 shorter events, 0.0 us)
Async XLA Ops:
  0.0 9.1 %collective-permute-start.2 = (bf16[64,2048]{1,0:T(8,128)(2,1)}, bf16[64,2048]{1,0:T(8,128)(2,1)S(1)}, u32[]{:S(2)}, u32[]{:S(2)}) collective-permute-start(bf16[64,2048]{1,0:T(8,128)(2,1)} %refs_0_.1), channel_id=1, source_target_pairs={{0,1},{1,0},{2,3},{3,2},{4,5},{5,4},{6,7},{7,6},{8,9},{9,8},{10,11... | collective-permute-start | bytes 786440 | tf_op jit(solution)/shard_map/ppermute | solution.py:219
  0.5 12.4 %collective-permute-start = (bf16[64,2048]{1,0:T(8,128)(2,1)}, bf16[64,2048]{1,0:T(8,128)(2,1)S(1)}, u32[]{:S(2)}, u32[]{:S(2)}) collective-permute-start(bf16[64,2048]{1,0:T(8,128)(2,1)} %refs_0_.1), channel_id=1, source_target_pairs={{2,0},{0,2},{3,1},{1,3},{6,4},{4,6},{7,5},{5,7},{10,8},{8,10},{11,... | collective-permute-start | bytes 786440 | tf_op jit(solution)/shard_map/ppermute | solution.py:222
  2.9 12.8 %collective-permute-start.1 = (bf16[64,2048]{1,0:T(8,128)(2,1)}, bf16[64,2048]{1,0:T(8,128)(2,1)S(1)}, u32[]{:S(2)}, u32[]{:S(2)}) collective-permute-start(bf16[64,2048]{1,0:T(8,128)(2,1)} %refs_2_.1), channel_id=1, source_target_pairs={{2,0},{0,2},{3,1},{1,3},{6,4},{4,6},{7,5},{5,7},{10,8},{8,10},{11,... | collective-permute-start | bytes 786440 | tf_op jit(solution)/shard_map/ppermute | solution.py:222
  3.0 13.2 %collective-permute-start.6 = (f32[16,4096]{1,0:T(8,128)}, f32[16,4096]{1,0:T(8,128)S(1)}, u32[]{:S(2)}, u32[]{:S(2)}) collective-permute-start(f32[16,4096]{1,0:T(8,128)} %refs_3_.1), channel_id=1, source_target_pairs={{4,0},{8,4},{12,8},{0,12},{13,1},{1,5},{5,9},{9,13},{6,2},{10,6},{... | collective-permute-start | bytes 786440 | tf_op jit(solution)/shard_map/ppermute | solution.py:198
  7.1 12.2 %collective-permute-start.8 = (f32[16,4096]{1,0:T(8,128)}, f32[16,4096]{1,0:T(8,128)S(1)}, u32[]{:S(2)}, u32[]{:S(2)}) collective-permute-start(f32[16,4096]{1,0:T(8,128)} %refs_3_.1), channel_id=1, source_target_pairs={{8,0},{12,4},{0,8},{4,12},{10,2},{14,6},{2,10},{6,14},{24,16},{28,... | collective-permute-start | bytes 786440 | tf_op jit(solution)/shard_map/ppermute | solution.py:204
  9.1 1.0 %copy-start.1 = (bf16[64,2048]{1,0:T(8,128)(2,1)S(1)}, bf16[64,2048]{1,0:T(8,128)(2,1)}, u32[]{:S(2)}) copy-start(bf16[64,2048]{1,0:T(8,128)(2,1)} %refs_0_.1) | copy-start | bytes 786436
  15.7 3.7 %collective-permute-start.5 = (bf16[64,2048]{1,0:T(8,128)(2,1)}, bf16[64,2048]{1,0:T(8,128)(2,1)S(1)}, u32[]{:S(2)}, u32[]{:S(2)}) collective-permute-start(bf16[64,2048]{1,0:T(8,128)(2,1)} %refs_2_.1), channel_id=1, source_target_pairs={{0,1},{1,0},{2,3},{3,2},{4,5},{5,4},{6,7},{7,6},{8,9},{9,8},{10,11... | collective-permute-start | bytes 786440 | tf_op jit(solution)/shard_map/ppermute | solution.py:219
  15.7 3.7 %collective-permute-start.3 = (bf16[64,2048]{1,0:T(8,128)(2,1)S(1)}, bf16[64,2048]{1,0:T(8,128)(2,1)S(1)}, u32[]{:S(2)}, u32[]{:S(2)}) collective-permute-start(bf16[64,2048]{1,0:T(8,128)(2,1)S(1)} %collective-permute-done.refs_0_), channel_id=1, source_target_pairs={{0,1},{1,0},{2,3},{3,2},{4,5},{5,4},{6,7},{7,6},{8,9},{9,8},{10,11... | collective-permute-start | bytes 786440 | tf_op jit(solution)/shard_map/ppermute | solution.py:219
  16.3 3.2 %collective-permute-start.4 = (bf16[64,2048]{1,0:T(8,128)(2,1)S(1)}, bf16[64,2048]{1,0:T(8,128)(2,1)S(1)}, u32[]{:S(2)}, u32[]{:S(2)}) collective-permute-start(bf16[64,2048]{1,0:T(8,128)(2,1)S(1)} %collective-permute-done.1.refs_1_), channel_id=1, source_target_pairs={{0,1},{1,0},{2,3},{3,2},{4,5},{5,4},{6,7},{7,6},{8,9},{9,8},{10,11... | collective-permute-start | bytes 786440 | tf_op jit(solution)/shard_map/ppermute | solution.py:219
  16.3 3.2 %collective-permute-start.7 = (f32[16,4096]{1,0:T(8,128)S(1)}, f32[16,4096]{1,0:T(8,128)S(1)}, u32[]{:S(2)}, u32[]{:S(2)}) collective-permute-start(f32[16,4096]{1,0:T(8,128)S(1)} %collective-permute-done.6.refs_4_), channel_id=1, source_target_pairs={{0,1},{1,0},{2,3},{3,2},{4,5},{5,4},{6,7},{7,6},{8,9},{9,8},{10,11... | collective-permute-start | bytes 786440 | tf_op jit(solution)/shard_map/ppermute | solution.py:219
  16.8 2.7 %copy-start = (f32[16,4096]{1,0:T(8,128)S(1)}, f32[16,4096]{1,0:T(8,128)}, u32[]{:S(2)}) copy-start(f32[16,4096]{1,0:T(8,128)} %refs_3_.1) | copy-start | bytes 786436
  16.8 2.7 %copy-start.2 = (s32[1,128]{1,0:T(1,128)S(1)}, s32[1,128]{1,0:T(1,128)}, u32[]{:S(2)}) copy-start(s32[1,128]{1,0:T(1,128)} %refs_8_.1) | copy-start | bytes 1540
  16.8 2.8 %copy-start.3 = (s32[1,128]{1,0:T(1,128)S(1)}, s32[1,128]{1,0:T(1,128)}, u32[]{:S(2)}) copy-start(s32[1,128]{1,0:T(1,128)} %refs_9_.1) | copy-start | bytes 1540
  19.3 3.9 %collective-permute-start.9 = (f32[16,4096]{1,0:T(8,128)S(1)}, f32[16,4096]{1,0:T(8,128)S(1)}, u32[]{:S(2)}, u32[]{:S(2)}) collective-permute-start(f32[16,4096]{1,0:T(8,128)S(1)} %collective-permute-done.8.here_ref), channel_id=1, source_target_pairs={{0,1},{1,0},{2,3},{3,2},{4,5},{5,4},{6,7},{7,6},{8,9},{9,8},{10,11... | collective-permute-start | bytes 786440 | tf_op jit(solution)/shard_map/ppermute | solution.py:219

commit v3 on v2

v3 whole, which is shorter than its diff:
```python
import jax
import jax.numpy as jnp
from jax import lax
from jax.experimental import pallas as pl
from jax.experimental.pallas import tpu as pltpu
from jax.sharding import PartitionSpec as P

TRAJ_DEV = 8
NT = (((1,), (1,)), ((), ()))
ANY = pl.BlockSpec(memory_space=pl.ANY)
VMEM = pl.BlockSpec(memory_space=pltpu.VMEM)
SMALL = pltpu.CompilerParams(vmem_limit_bytes=8 << 20)
PARAMS = pltpu.CompilerParams(vmem_limit_bytes=52 << 20)


def dot_nt(a, b):
    return lax.dot_general(a, b, NT, preferred_element_type=jnp.float32)


def halves(a):
    high = a.astype(jnp.bfloat16)
    return high, (a - high.astype(jnp.float32)).astype(jnp.bfloat16)


class Chunks:
    def __init__(self, toks_hbm, owners, projs, toks, sems, first):
        self.toks, self.projs, self.first, self.copies = toks, projs, first, []
        width = toks.shape[2]
        for i, owner in enumerate(owners):
            columns = pl.ds(pl.multiple_of(owner * width, 128), width)
            copy = pltpu.make_async_copy(
                toks_hbm.at[:, columns], toks.at[first + i], sems.at[first + i]
            )
            copy.start()
            self.copies.append(copy)

    def total(self, base):
        for i, copy in enumerate(self.copies):
            copy.wait()
            part = dot_nt(self.toks[self.first + i], self.projs[i][...])
            base = part if base is None else base + part
        return base


def chunk_scratch(n, toks, projs):
    return [
        pltpu.VMEM((n, toks.shape[0], projs[0].shape[1]), toks.dtype),
        pltpu.SemaphoreType.DMA((n,)),
    ]


def project(sides, table, bases):
    rank, width = sides[0][1][0].shape
    count = sides[0][0].shape[0]
    n, total = len(sides), sum(len(projs) for _, projs, _ in sides)

    def kernel(*refs):
        table_ref = table()
        toks, refs = refs[:n], refs[n:]
        proj_hbm, refs = refs[:total], refs[total:]
        base_refs, refs = refs[: len(bases)], refs[len(bases) :]
        out_refs, scratch = refs[:n], refs[n:]
        first, chunks = 0, []
        for tok, (_, projs, places) in zip(toks, sides):
            last = first + len(projs)
            owners = [table_ref[place] for place in places]
            chunks.append(Chunks(tok, owners, proj_hbm[first:last], *scratch, first))
            first = last
        for i, (chunk, out_ref) in enumerate(zip(chunks, out_refs)):
            out_ref[...] = chunk.total(base_refs[i][...] if i < len(bases) else None)

    shapes = [jax.ShapeDtypeStruct((count, rank), jnp.float32)] * n
    scratch = chunk_scratch(total, sides[0][0], sides[0][1])
    return pl.pallas_call(
        kernel,
        out_shape=shapes,
        in_specs=[ANY] * n + [VMEM] * (total + len(bases)),
        out_specs=[VMEM] * n,
        scratch_shapes=scratch,
        compiler_params=PARAMS,
        cost_estimate=cost(),
    )(*[side[0] for side in sides], *[p for side in sides for p in side[1]], *bases)


def partial_scores(q_halves, f_stack):
    q_high, q_low = q_halves
    both = dot_nt(f_stack, q_high)
    return both[:TRAJ_DEV] + both[TRAJ_DEV:] + dot_nt(f_stack, q_low)[:TRAJ_DEV]


def spread_blocks(scores, places, slots):
    rows = scores.shape[1] // len(places)
    block = lax.broadcasted_iota(jnp.int32, (TRAJ_DEV, rows * slots), 1) // rows
    ordered = jnp.zeros((TRAJ_DEV, rows * slots), jnp.float32)
    for s, place in enumerate(places):
        piece = scores[:, s * rows : (s + 1) * rows]
        ordered = jnp.where(block == place, jnp.concatenate([piece] * slots, axis=1), ordered)
    return ordered


def gradients(
    table, in_side, out_side, bases, segments, loss_mask, numbered, pieces, slots
):
    count, rank = bases[0].shape
    rows, flat_width = pieces[0].shape
    acts, in_projs, in_places = in_side
    grads, out_projs, out_places = out_side
    n, m, k = len(in_projs), len(out_projs), len(pieces)

    def kernel(act, grad, *refs):
        table_ref = table()
        proj_hbm, piece_refs, refs = refs[: n + m], refs[n + m : n + m + k], refs[n + m + k :]
        in_base, out_base, seg_ref, mask_ref, stack_ref, score_ref = refs[:6]
        scratch = refs[6:]
        ins = Chunks(act, [table_ref[p] for p in in_places], proj_hbm[:n], *scratch, 0)
        outs = Chunks(grad, [table_ref[p] for p in out_places], proj_hbm[n:], *scratch, n)
        q_halves = halves(jnp.concatenate([ref[...] for ref in piece_refs], axis=0))
        own = seg_ref[...] == lax.broadcasted_iota(jnp.int32, (TRAJ_DEV, count), 0)
        masked = jnp.where(own, mask_ref[...].astype(jnp.float32), 0.0)
        counts = jnp.sum(masked, axis=1, keepdims=True)
        weight = masked * (1.0 / jnp.maximum(counts, 1.0))
        in_t = ins.total(in_base[...]).T
        t_high, t_low = halves(jnp.concatenate([in_t, in_t], axis=0))
        out_t = outs.total(out_base[...]).T
        left = (out_t[:, None, :] * weight[None]).reshape(rank * TRAJ_DEV, count)
        l_high, l_low = halves(left)
        outer = dot_nt(
            jnp.concatenate([l_high, l_low], axis=1), jnp.concatenate([t_high, t_high], axis=1)
        ) + dot_nt(l_high, t_low)
        outer = outer.reshape(rank // 2, 2, TRAJ_DEV, 2 * rank)
        low = lax.broadcasted_iota(jnp.int32, (TRAJ_DEV, 2 * rank), 1) < rank
        flat = jnp.concatenate(
            [jnp.where(low, outer[p, 0], outer[p, 1]) for p in range(rank // 2)], axis=1
        )
        f_stack = jnp.concatenate(halves(flat), axis=0)
        scores = partial_scores(q_halves, f_stack)
        stack_ref[...] = f_stack
        score_ref[...] = spread_blocks(scores, [table_ref[p] for p in numbered], slots)

    return pl.pallas_call(
        kernel,
        out_shape=(
            jax.ShapeDtypeStruct((2 * TRAJ_DEV, flat_width), jnp.bfloat16),
            jax.ShapeDtypeStruct((TRAJ_DEV, rows * slots), jnp.float32),
        ),
        in_specs=[ANY] * 2 + [VMEM] * (n + m + k + 4),
        out_specs=(VMEM, VMEM),
        scratch_shapes=chunk_scratch(n + m, acts, in_projs),
        compiler_params=PARAMS,
        cost_estimate=cost(),
    )(
        acts,
        grads,
        *in_projs,
        *out_projs,
        *pieces,
        *bases,
        segments,
        loss_mask,
    )


def last_block(table, numbered, scores, f_stack, here, there):
    slots = scores.shape[1] // here.shape[0]

    def kernel(base_ref, stack_ref, here_ref, there_ref, score_ref):
        table_ref = table()
        block = jnp.where(table_ref[numbered[1]] == 0, here_ref[...], there_ref[...])
        scores = partial_scores(halves(block), stack_ref[...])
        score_ref[...] = base_ref[...] + spread_blocks(scores, [table_ref[numbered[0]]], slots)

    return pl.pallas_call(
        kernel,
        out_shape=jax.ShapeDtypeStruct(scores.shape, jnp.float32),
        in_specs=[VMEM] * 4,
        out_specs=VMEM,
        compiler_params=SMALL,
        cost_estimate=cost(),
    )(scores, f_stack, here, there)


def cost():
    return pl.CostEstimate(flops=1, bytes_accessed=1, transcendentals=0)


def fetch_queries(queries, sizes):
    n = sizes["traj"]
    if n != 4:
        return [lax.all_gather(queries, "traj", axis=0, tiled=True)]
    line = range(n)
    beside = lax.ppermute(
        queries,
        ("traj", "sub"),
        [(2 * ((z + 1) % n), 2 * z) for z in line]
        + [(2 * ((z + n - 1) % n) + 1, 2 * z + 1) for z in line],
    )
    across = lax.ppermute(queries, ("traj", "sub"), [(2 * ((z + 2) % n), 2 * z) for z in line])
    return [beside, across]


def body(sizes, activations, out_grads, segments, loss_mask, proj_in, proj_out, queries):
    chips = sizes["fsdp"]

    def to_core(a):
        return lax.ppermute(a, "sub", [(0, 1), (1, 0)])

    def from_chip(a, d):
        return lax.ppermute(a, "fsdp", [((i + d) % chips, i) for i in range(chips)])

    def after(arrays, *waited):
        return lax.optimization_barrier((arrays, *waited))

    far_in = [from_chip(proj_in, d) for d in range(1, chips)]
    far_out = [from_chip(proj_out, d) for d in range(1, chips)]
    fetched = fetch_queries(queries, sizes)
    on_line = len(fetched) > 1

    far_own, far_other = [2 * d for d in range(1, chips)], [2 * d + 1 for d in range(1, chips)]
    numbered = [2 * chips + s for s in range(5)]

    def table():
        x, core = lax.axis_index("fsdp"), lax.axis_index("sub")
        chunks = [2 * lax.rem(x + d, chips) + c for d in range(chips) for c in (core, 1 - core)]
        if not on_line:
            return chunks + [0]
        at, step = lax.axis_index("traj"), 1 + 2 * core
        blocks = [at, at + step, at + 4 - step, at + 2]
        return chunks + [lax.rem(b, 4) for b in blocks] + [core]

    in_sum, out_sum = project(
        [(activations, [proj_in, to_core(proj_in)], [0, 1]), (out_grads, [proj_out], [0])],
        table,
        [],
    )
    far_in, late_out, in_sum, out_sum = after(far_in, proj_out, in_sum, out_sum)
    others_in = [to_core(a) for a in far_in]
    other_out = to_core(late_out)
    (in_sum,) = project([(activations, far_in, far_own)], table, [in_sum])
    if on_line:
        beside, across = fetched
        beside, in_sum = after(beside, in_sum)
        beside_other = to_core(beside)
    else:
        pieces = fetched
    far_out, beside, in_sum = after(far_out, beside if on_line else in_sum, in_sum)
    others_out = [to_core(a) for a in far_out] + [other_out]
    if on_line:
        pieces = [queries, beside, beside_other]
    (out_sum,) = project([(out_grads, far_out, far_own)], table, [out_sum])
    if on_line:
        across, out_sum = after(across, out_sum)
        across_other = to_core(across)
    f_stack, scores = gradients(
        table,
        (activations, others_in, far_other),
        (out_grads, others_out, far_other + [1]),
        (in_sum, out_sum),
        segments,
        loss_mask,
        numbered[: len(pieces)],
        pieces,
        4 if on_line else 1,
    )
    if on_line:
        scores = last_block(table, numbered[3:], scores, f_stack, across, across_other)
    return scores.T


def solution(mesh):
    placed = (
        P(("groups", "traj", "fsdp", "sub"), None),
        P(("groups", "traj", "fsdp", "sub"), None),
        P(("groups", "traj", "fsdp", "sub"), None),
        P(("groups", "traj", "fsdp", "sub"), None),
        P(None, ("fsdp", "sub")),
        P(None, ("fsdp", "sub")),
        P(("groups", "traj"), None),
    )
    sizes = dict(mesh.shape)

    def program(*arrays):
        return body(sizes, *arrays)

    return jax.shard_map(
        program,
        mesh=mesh,
        in_specs=placed,
        out_specs=P("groups", ("traj", "fsdp", "sub")),
        check_vma=False,
    )
```

time: 25 us -> 23.4 us (0.936)
  waiting for transfers between devices: 3.76 us -> 2.11 us
  Pallas kernels: 9.6 us -> 8.71 us
  local copies, waits for them, and re-layouts: 1.05 us -> 1.91 us
    ppermute x2, waiting for transfers between devices: 2.92 us -> 0.62 us  [from_chip(): return lax.ppermute(a, 'fsdp', [((i + d) % chips, i) for i in range(chips)])]
    unnamed x8 -> x10, local copies, waits for them, and re-layouts: 0.96 us -> 1.91 us
    pallas_call x1, Pallas kernels: 3.67 us -> 2.94 us  [gradients(): pl.pallas_call(kernel, out_shape=(jax.ShapeDtypeStruct((2 * TRAJ_DEV, fla...]
    ppermute x1, waiting for transfers between devices: 0.82 us -> 1.47 us  [fetch_queries(): lax.ppermute(queries, ('traj', 'sub'), [(2 * ((z + 2) % n), 2 * z) for z...]
    pallas_call x1, Pallas kernels: 1.45 us -> 0.91 us  [last_block(): pl.pallas_call(kernel, out_shape=jax.ShapeDtypeStruct(scores.shape, jnp.f...]
    ppermute x2, starting transfers between devices: 2.56 us -> 3.02 us  [from_chip(): return lax.ppermute(a, 'fsdp', [((i + d) % chips, i) for i in range(chips)])]
    ppermute x1, starting transfers between devices: 4.07 us -> 3.6 us  [fetch_queries(): lax.ppermute(queries, ('traj', 'sub'), [(2 * ((z + 1) % n), 2 * z) for z...]
    pallas_call x2 -> x3, Pallas kernels: 4.48 us -> 4.86 us  [project(): pl.pallas_call(kernel, out_shape=shapes, in_specs=[ANY] * n + [VMEM] * (t...]
  transfers between devices with their start and end apart: 10 -> 10, of which waited for: 2 -> 2; matrix products, arithmetic and copies ran while one was open for 1% -> 0% of each run, Pallas kernels for 33% -> 34%
where the time goes in v3:
time: 23.4 us; the launch traced here: 23 us
  starting transfers between devices  10.1 us (43%)
  Pallas kernels  8.71 us (37%)
  waiting for transfers between devices  2.11 us (9%)
  local copies, waits for them, and re-layouts  1.91 us (8%)
    pallas_call x3, Pallas kernels, project(): pl.pallas_call(kernel, out_shape=shapes, in_specs=[ANY] * n + [VMEM] * (t...  4.86 us
    ppermute x1, starting transfers between devices, fetch_queries(): lax.ppermute(queries, ('traj', 'sub'), [(2 * ((z + 1) % n), 2 * z) for z...  3.6 us
    ppermute x2, starting transfers between devices, from_chip(): return lax.ppermute(a, 'fsdp', [((i + d) % chips, i) for i in range(chips)])  3.02 us
    pallas_call x1, Pallas kernels, gradients(): pl.pallas_call(kernel, out_shape=(jax.ShapeDtypeStruct((2 * TRAJ_DEV, fla...  2.94 us
    unnamed x10, local copies, waits for them, and re-layouts  1.91 us
    ppermute x1, starting transfers between devices, fetch_queries(): lax.ppermute(queries, ('traj', 'sub'), [(2 * ((z + 2) % n), 2 * z) for z...  1.91 us
    ppermute x6, starting transfers between devices, to_core(): return lax.ppermute(a, 'sub', [(0, 1), (1, 0)])  1.59 us
    ppermute x1, waiting for transfers between devices, fetch_queries(): lax.ppermute(queries, ('traj', 'sub'), [(2 * ((z + 2) % n), 2 * z) for z...  1.47 us
  transfers between devices with their start and end apart: 10, of which 2 were waited for; matrix products, arithmetic and copies ran while one was open for 0% of the time, Pallas kernels for 34%

profile of v3, /device:TPU:0, one launch (start us, length us, event | category | flops | bytes accessed | tf_op | source)
XLA Modules:
  0.0 23.0 jit_solution(2880069392939462071)
XLA Ops:
  0.0 0.5 %collective-permute-start.1 = (bf16[64,2048]{1,0:T(8,128)(2,1)}, bf16[64,2048]{1,0:T(8,128)(2,1)S(1)}, u32[]{:S(2)}, u32[]{:S(2)}) collective-permute-start(bf16[64,2048]{1,0:T(8,128)(2,1)} %refs_2_.1), channel_id=1, source_target_pairs={{0,1},{1,0},{2,3},{3,2},{4,5},{5,4},{6,7},{7,6},{8,9},{9,8},{10,11... | collective-permute-start | bytes 786440 | tf_op jit(solution)/shard_map/ppermute | solution.py:205
  0.5 2.5 %collective-permute-start = (bf16[64,2048]{1,0:T(8,128)(2,1)}, bf16[64,2048]{1,0:T(8,128)(2,1)S(1)}, u32[]{:S(2)}, u32[]{:S(2)}) collective-permute-start(bf16[64,2048]{1,0:T(8,128)(2,1)} %refs_2_.1), channel_id=1, source_target_pairs={{2,0},{0,2},{3,1},{1,3},{6,4},{4,6},{7,5},{5,7},{10,8},{8,10},{11,... | collective-permute-start | bytes 786440 | tf_op jit(solution)/shard_map/ppermute | solution.py:208
  2.9 3.6 %collective-permute-start.4 = (f32[16,4096]{1,0:T(8,128)}, f32[16,4096]{1,0:T(8,128)S(1)}, u32[]{:S(2)}, u32[]{:S(2)}) collective-permute-start(f32[16,4096]{1,0:T(8,128)} %refs_3_.1), channel_id=1, source_target_pairs={{4,0},{8,4},{12,8},{0,12},{13,1},{1,5},{5,9},{9,13},{6,2},{10,6},{... | collective-permute-start | bytes 786440 | tf_op jit(solution)/shard_map/ppermute | solution.py:191
  6.5 0.5 %collective-permute-start.3 = (bf16[64,2048]{1,0:T(8,128)(2,1)}, bf16[64,2048]{1,0:T(8,128)(2,1)S(1)}, u32[]{:S(2)}, u32[]{:S(2)}) collective-permute-start(bf16[64,2048]{1,0:T(8,128)(2,1)} %refs_4_.1), channel_id=1, source_target_pairs={{2,0},{0,2},{3,1},{1,3},{6,4},{4,6},{7,5},{5,7},{10,8},{8,10},{11,... | collective-permute-start | bytes 786440 | tf_op jit(solution)/shard_map/ppermute | solution.py:208
  7.1 1.9 %collective-permute-start.8 = (f32[16,4096]{1,0:T(8,128)}, f32[16,4096]{1,0:T(8,128)S(1)}, u32[]{:S(2)}, u32[]{:S(2)}) collective-permute-start(f32[16,4096]{1,0:T(8,128)} %refs_3_.1), channel_id=1, source_target_pairs={{8,0},{12,4},{0,8},{4,12},{10,2},{14,6},{2,10},{6,14},{24,16},{28,... | collective-permute-start | bytes 786440 | tf_op jit(solution)/shard_map/ppermute | solution.py:197
  9.0 0.0 collective-permute-done.1.refs_3_
  9.0 0.0 copy-start
  9.0 0.9 %copy-done = bf16[64,2048]{1,0:T(8,128)(2,1)S(1)} copy-done((bf16[64,2048]{1,0:T(8,128)(2,1)S(1)}, bf16[64,2048]{1,0:T(8,128)(2,1)}, u32[]{:S(2)}) %copy-start) | copy-done | bytes 262168
  10.0 0.9 %copy-done.1 = bf16[64,2048]{1,0:T(8,128)(2,1)S(1)} copy-done((bf16[64,2048]{1,0:T(8,128)(2,1)S(1)}, bf16[64,2048]{1,0:T(8,128)(2,1)}, u32[]{:S(2)}) %copy-start.1) | copy-done | bytes 262168
  10.9 2.2 %shard_map.73 = (f32[128,64]{1,0:T(8,128)S(1)}, f32[128,64]{1,0:T(8,128)S(1)}) custom-call(bf16[128,8192]{1,0:T(8,128)(2,1)} %act.1, bf16[128,8192]{1,0:T(8,128)(2,1)} %grad.1, bf16[64,2048]{1,0:T(8,128)(2,1)S(1)} %copy-done, bf16[64,2048]{1,0:T(8,128)(2,1)S(1)} %collective-permute-done.1.refs_3_, bf16[64,2048]{1,0:T(8,128)(2,1)S(1)} %copy-done.1), custom_call_target="tpu_custom_call" | custom-call | flops 1 | bytes 1 | tf_op jit(solution)/shard_map/pallas_call | solution.py:74
  13.1 0.0 collective-permute-done.refs_1_
  13.1 0.0 copy-start.2
  13.1 0.0 copy-start.3
  13.1 0.0 copy-start.4
  13.1 0.1 collective-permute-start.2
  13.2 1.4 %shard_map.74.refs_6_ = f32[128,64]{1,0:T(8,128)S(1)} custom-call(bf16[128,8192]{1,0:T(8,128)(2,1)} %act.1, bf16[64,2048]{1,0:T(8,128)(2,1)S(1)} %collective-permute-done.refs_1_, f32[128,64]{1,0:T(8,128)S(1)} %get-tuple-element.23.refs_2_), custom_call_target="tpu_custom_call" | custom-call | flops 1 | bytes 1 | tf_op jit(solution)/shard_map/pallas_call | solution.py:74
  14.6 0.6 %collective-permute-start.6 = (bf16[64,2048]{1,0:T(8,128)(2,1)S(1)}, bf16[64,2048]{1,0:T(8,128)(2,1)S(1)}, u32[]{:S(2)}, u32[]{:S(2)}) collective-permute-start(bf16[64,2048]{1,0:T(8,128)(2,1)S(1)} %copy-done.1), channel_id=1, source_target_pairs={{0,1},{1,0},{2,3},{3,2},{4,5},{5,4},{6,7},{7,6},{8,9},{9,8},{10,11... | collective-permute-start | bytes 786440 | tf_op jit(solution)/shard_map/ppermute | solution.py:205
  15.1 0.0 collective-permute-done.4.refs_4_
  15.1 0.6 %collective-permute-done.3.refs_1_ = bf16[64,2048]{1,0:T(8,128)(2,1)S(1)} collective-permute-done((bf16[64,2048]{1,0:T(8,128)(2,1)}, bf16[64,2048]{1,0:T(8,128)(2,1)S(1)}, u32[]{:S(2)}, u32[]{:S(2)}) %collective-permute-start.3) | collective-permute-done | bytes 262176 | tf_op jit(solution)/shard_map/ppermute | solution.py:208
  15.7 0.0 collective-permute-start.5
  15.7 0.5 %collective-permute-start.7 = (f32[16,4096]{1,0:T(8,128)S(1)}, f32[16,4096]{1,0:T(8,128)S(1)}, u32[]{:S(2)}, u32[]{:S(2)}) collective-permute-start(f32[16,4096]{1,0:T(8,128)S(1)} %collective-permute-done.4.refs_4_), channel_id=1, source_target_pairs={{0,1},{1,0},{2,3},{3,2},{4,5},{5,4},{6,7},{7,6},{8,9},{9,8},{10,11... | collective-permute-start | bytes 786440 | tf_op jit(solution)/shard_map/ppermute | solution.py:205
  16.3 1.3 %shard_map.75.refs_7_ = f32[128,64]{1,0:T(8,128)S(1)} custom-call(bf16[128,8192]{1,0:T(8,128)(2,1)} %grad.1, bf16[64,2048]{1,0:T(8,128)(2,1)S(1)} %collective-permute-done.3.refs_1_, f32[128,64]{1,0:T(8,128)S(1)} %get-tuple-element.30.refs_2_), custom_call_target="tpu_custom_call" | custom-call | flops 1 | bytes 1 | tf_op jit(solution)/shard_map/pallas_call | solution.py:74
  17.6 1.5 %collective-permute-done.8.here_ref = f32[16,4096]{1,0:T(8,128)S(1)} collective-permute-done((f32[16,4096]{1,0:T(8,128)}, f32[16,4096]{1,0:T(8,128)S(1)}, u32[]{:S(2)}, u32[]{:S(2)}) %collective-permute-start.8) | collective-permute-done | bytes 262176 | tf_op jit(solution)/shard_map/ppermute | solution.py:197
  19.1 0.0 collective-permute-start.9
  19.1 0.0 collective-permute-done.6.refs_2_
  19.1 0.0 collective-permute-done.2.refs_0_
  19.1 0.0 collective-permute-done.5.refs_1_
  19.1 0.0 collective-permute-done.7.refs_5_
  19.1 0.0 copy-done.2
  19.1 2.9 %shard_map.76 = (bf16[16,4096]{1,0:T(8,128)(2,1)S(1)}, f32[8,64]{1,0:T(8,128)S(1)}) custom-call(bf16[128,8192]{1,0:T(8,128)(2,1)} %act.1, bf16[128,8192]{1,0:T(8,128)(2,1)} %grad.1, bf16[64,2048]{1,0:T(8,128)(2,1)S(1)} %collective-permute-done.2.refs_0_, bf16[64,2048]{1,0:T(8,128)(2,1)S(1)} %collective-permute-done.5.refs_1_, ...), custom_call_target="tpu_custom_call" | custom-call | flops 1 | bytes 1 | tf_op jit(solution)/shard_map/pallas_call | solution.py:140
  22.1 0.0 collective-permute-done.9.there_ref
  22.1 0.9 %shard_map.77 = f32[8,64]{1,0:T(8,128)} custom-call(f32[8,64]{1,0:T(8,128)S(1)} %get-tuple-element.32.base_ref, bf16[16,4096]{1,0:T(8,128)(2,1)S(1)} %get-tuple-element.33.stack_ref, f32[16,4096]{1,0:T(8,128)S(1)} %collective-permute-done.8.here_ref, f32[16,4096]{1,0:T(8,128)S(1)} %collective-permute-done.9.there_ref), custom_call_target="tpu_custom_call" | custom-call | flops 1 | bytes 1 | tf_op jit(solution)/shard_map/pallas_call | solution.py:172
  (3 shorter events, 0.0 us)
Async XLA Ops:
  0.0 9.0 %collective-permute-start.1 = (bf16[64,2048]{1,0:T(8,128)(2,1)}, bf16[64,2048]{1,0:T(8,128)(2,1)S(1)}, u32[]{:S(2)}, u32[]{:S(2)}) collective-permute-start(bf16[64,2048]{1,0:T(8,128)(2,1)} %refs_2_.1), channel_id=1, source_target_pairs={{0,1},{1,0},{2,3},{3,2},{4,5},{5,4},{6,7},{7,6},{8,9},{9,8},{10,11... | collective-permute-start | bytes 786440 | tf_op jit(solution)/shard_map/ppermute | solution.py:205
  0.5 12.6 %collective-permute-start = (bf16[64,2048]{1,0:T(8,128)(2,1)}, bf16[64,2048]{1,0:T(8,128)(2,1)S(1)}, u32[]{:S(2)}, u32[]{:S(2)}) collective-permute-start(bf16[64,2048]{1,0:T(8,128)(2,1)} %refs_2_.1), channel_id=1, source_target_pairs={{2,0},{0,2},{3,1},{1,3},{6,4},{4,6},{7,5},{5,7},{10,8},{8,10},{11,... | collective-permute-start | bytes 786440 | tf_op jit(solution)/shard_map/ppermute | solution.py:208
  2.9 12.2 %collective-permute-start.4 = (f32[16,4096]{1,0:T(8,128)}, f32[16,4096]{1,0:T(8,128)S(1)}, u32[]{:S(2)}, u32[]{:S(2)}) collective-permute-start(f32[16,4096]{1,0:T(8,128)} %refs_3_.1), channel_id=1, source_target_pairs={{4,0},{8,4},{12,8},{0,12},{13,1},{1,5},{5,9},{9,13},{6,2},{10,6},{... | collective-permute-start | bytes 786440 | tf_op jit(solution)/shard_map/ppermute | solution.py:191
  6.5 9.2 %collective-permute-start.3 = (bf16[64,2048]{1,0:T(8,128)(2,1)}, bf16[64,2048]{1,0:T(8,128)(2,1)S(1)}, u32[]{:S(2)}, u32[]{:S(2)}) collective-permute-start(bf16[64,2048]{1,0:T(8,128)(2,1)} %refs_4_.1), channel_id=1, source_target_pairs={{2,0},{0,2},{3,1},{1,3},{6,4},{4,6},{7,5},{5,7},{10,8},{8,10},{11,... | collective-permute-start | bytes 786440 | tf_op jit(solution)/shard_map/ppermute | solution.py:208
  7.1 12.0 %collective-permute-start.8 = (f32[16,4096]{1,0:T(8,128)}, f32[16,4096]{1,0:T(8,128)S(1)}, u32[]{:S(2)}, u32[]{:S(2)}) collective-permute-start(f32[16,4096]{1,0:T(8,128)} %refs_3_.1), channel_id=1, source_target_pairs={{8,0},{12,4},{0,8},{4,12},{10,2},{14,6},{2,10},{6,14},{24,16},{28,... | collective-permute-start | bytes 786440 | tf_op jit(solution)/shard_map/ppermute | solution.py:197
  9.0 1.0 %copy-start = (bf16[64,2048]{1,0:T(8,128)(2,1)S(1)}, bf16[64,2048]{1,0:T(8,128)(2,1)}, u32[]{:S(2)}) copy-start(bf16[64,2048]{1,0:T(8,128)(2,1)} %refs_2_.1) | copy-start | bytes 786436
  10.0 0.9 %copy-start.1 = (bf16[64,2048]{1,0:T(8,128)(2,1)S(1)}, bf16[64,2048]{1,0:T(8,128)(2,1)}, u32[]{:S(2)}) copy-start(bf16[64,2048]{1,0:T(8,128)(2,1)} %refs_4_.1) | copy-start | bytes 786436
  13.1 6.0 %copy-start.2 = (f32[16,4096]{1,0:T(8,128)S(1)}, f32[16,4096]{1,0:T(8,128)}, u32[]{:S(2)}) copy-start(f32[16,4096]{1,0:T(8,128)} %refs_3_.1) | copy-start | bytes 786436
  13.1 6.0 %copy-start.3 = (s32[1,128]{1,0:T(1,128)S(1)}, s32[1,128]{1,0:T(1,128)}, u32[]{:S(2)}) copy-start(s32[1,128]{1,0:T(1,128)} %refs_8_.1) | copy-start | bytes 1540
  13.1 6.0 %copy-start.4 = (s32[1,128]{1,0:T(1,128)S(1)}, s32[1,128]{1,0:T(1,128)}, u32[]{:S(2)}) copy-start(s32[1,128]{1,0:T(1,128)} %refs_9_.1) | copy-start | bytes 1540
  13.1 5.9 %collective-permute-start.2 = (bf16[64,2048]{1,0:T(8,128)(2,1)S(1)}, bf16[64,2048]{1,0:T(8,128)(2,1)S(1)}, u32[]{:S(2)}, u32[]{:S(2)}) collective-permute-start(bf16[64,2048]{1,0:T(8,128)(2,1)S(1)} %collective-permute-done.refs_1_), channel_id=1, source_target_pairs={{0,1},{1,0},{2,3},{3,2},{4,5},{5,4},{6,7},{7,6},{8,9},{9,8},{10,11... | collective-permute-start | bytes 786440 | tf_op jit(solution)/shard_map/ppermute | solution.py:205
  14.6 4.5 %collective-permute-start.6 = (bf16[64,2048]{1,0:T(8,128)(2,1)S(1)}, bf16[64,2048]{1,0:T(8,128)(2,1)S(1)}, u32[]{:S(2)}, u32[]{:S(2)}) collective-permute-start(bf16[64,2048]{1,0:T(8,128)(2,1)S(1)} %copy-done.1), channel_id=1, source_target_pairs={{0,1},{1,0},{2,3},{3,2},{4,5},{5,4},{6,7},{7,6},{8,9},{9,8},{10,11... | collective-permute-start | bytes 786440 | tf_op jit(solution)/shard_map/ppermute | solution.py:205
  15.7 3.3 %collective-permute-start.5 = (bf16[64,2048]{1,0:T(8,128)(2,1)S(1)}, bf16[64,2048]{1,0:T(8,128)(2,1)S(1)}, u32[]{:S(2)}, u32[]{:S(2)}) collective-permute-start(bf16[64,2048]{1,0:T(8,128)(2,1)S(1)} %collective-permute-done.3.refs_1_), channel_id=1, source_target_pairs={{0,1},{1,0},{2,3},{3,2},{4,5},{5,4},{6,7},{7,6},{8,9},{9,8},{10,11... | collective-permute-start | bytes 786440 | tf_op jit(solution)/shard_map/ppermute | solution.py:205
  15.7 3.3 %collective-permute-start.7 = (f32[16,4096]{1,0:T(8,128)S(1)}, f32[16,4096]{1,0:T(8,128)S(1)}, u32[]{:S(2)}, u32[]{:S(2)}) collective-permute-start(f32[16,4096]{1,0:T(8,128)S(1)} %collective-permute-done.4.refs_4_), channel_id=1, source_target_pairs={{0,1},{1,0},{2,3},{3,2},{4,5},{5,4},{6,7},{7,6},{8,9},{9,8},{10,11... | collective-permute-start | bytes 786440 | tf_op jit(solution)/shard_map/ppermute | solution.py:205
  19.1 3.0 %collective-permute-start.9 = (f32[16,4096]{1,0:T(8,128)S(1)}, f32[16,4096]{1,0:T(8,128)S(1)}, u32[]{:S(2)}, u32[]{:S(2)}) collective-permute-start(f32[16,4096]{1,0:T(8,128)S(1)} %collective-permute-done.8.here_ref), channel_id=1, source_target_pairs={{0,1},{1,0},{2,3},{3,2},{4,5},{5,4},{6,7},{7,6},{8,9},{9,8},{10,11... | collective-permute-start | bytes 786440 | tf_op jit(solution)/shard_map/ppermute | solution.py:205

commit v4 on v3

--- a/solution.py
+++ b/solution.py
@@ -82,6 +82,25 @@
     )(*[side[0] for side in sides], *[p for side in sides for p in side[1]], *bases)
 
 
+def add_chunks(base, toks, projs):
+    n = len(toks)
+
+    def kernel(base_ref, *refs):
+        total = base_ref[...]
+        for tok, proj in zip(refs[:n], refs[n : 2 * n]):
+            total = total + dot_nt(tok[...], proj[...])
+        refs[2 * n][...] = total
+
+    return pl.pallas_call(
+        kernel,
+        out_shape=jax.ShapeDtypeStruct(base.shape, base.dtype),
+        in_specs=[VMEM] * (1 + 2 * n),
+        out_specs=VMEM,
+        compiler_params=SMALL,
+        cost_estimate=cost(),
+    )(base, *toks, *projs)
+
+
 def partial_scores(q_halves, f_stack):
     q_high, q_low = q_halves
     both = dot_nt(f_stack, q_high)
@@ -103,25 +122,24 @@
 ):
     count, rank = bases[0].shape
     rows, flat_width = pieces[0].shape
-    acts, in_projs, in_places = in_side
-    grads, out_projs, out_places = out_side
+    acts, in_projs = in_side
+    grads, out_projs = out_side
     n, m, k = len(in_projs), len(out_projs), len(pieces)
 
-    def kernel(act, grad, *refs):
+    def kernel(*refs):
         table_ref = table()
-        proj_hbm, piece_refs, refs = refs[: n + m], refs[n + m : n + m + k], refs[n + m + k :]
-        in_base, out_base, seg_ref, mask_ref, stack_ref, score_ref = refs[:6]
-        scratch = refs[6:]
-        ins = Chunks(act, [table_ref[p] for p in in_places], proj_hbm[:n], *scratch, 0)
-        outs = Chunks(grad, [table_ref[p] for p in out_places], proj_hbm[n:], *scratch, n)
+        tok_refs, refs = refs[: n + m], refs[n + m :]
+        proj_refs, piece_refs, refs = refs[: n + m], refs[n + m : n + m + k], refs[n + m + k :]
+        parts = [dot_nt(tok[...], proj[...]) for tok, proj in zip(tok_refs, proj_refs)]
+        in_base, out_base, seg_ref, mask_ref, stack_ref, score_ref = refs
         q_halves = halves(jnp.concatenate([ref[...] for ref in piece_refs], axis=0))
         own = seg_ref[...] == lax.broadcasted_iota(jnp.int32, (TRAJ_DEV, count), 0)
         masked = jnp.where(own, mask_ref[...].astype(jnp.float32), 0.0)
         counts = jnp.sum(masked, axis=1, keepdims=True)
         weight = masked * (1.0 / jnp.maximum(counts, 1.0))
-        in_t = ins.total(in_base[...]).T
+        in_t = sum(parts[:n], in_base[...]).T
         t_high, t_low = halves(jnp.concatenate([in_t, in_t], axis=0))
-        out_t = outs.total(out_base[...]).T
+        out_t = sum(parts[n:], out_base[...]).T
         left = (out_t[:, None, :] * weight[None]).reshape(rank * TRAJ_DEV, count)
         l_high, l_low = halves(left)
         outer = dot_nt(
@@ -143,14 +161,13 @@
             jax.ShapeDtypeStruct((2 * TRAJ_DEV, flat_width), jnp.bfloat16),
             jax.ShapeDtypeStruct((TRAJ_DEV, rows * slots), jnp.float32),
         ),
-        in_specs=[ANY] * 2 + [VMEM] * (n + m + k + 4),
+        in_specs=[VMEM] * (2 * (n + m) + k + 4),
         out_specs=(VMEM, VMEM),
-        scratch_shapes=chunk_scratch(n + m, acts, in_projs),
-        compiler_params=PARAMS,
+        compiler_params=SMALL,
         cost_estimate=cost(),
     )(
-        acts,
-        grads,
+        *acts,
+        *grads,
         *in_projs,
         *out_projs,
         *pieces,
@@ -199,7 +216,7 @@
 
 
 def body(sizes, activations, out_grads, segments, loss_mask, proj_in, proj_out, queries):
-    chips = sizes["fsdp"]
+    chips, width = sizes["fsdp"], proj_in.shape[1]
 
     def to_core(a):
         return lax.ppermute(a, "sub", [(0, 1), (1, 0)])
@@ -242,18 +259,33 @@
         beside_other = to_core(beside)
     else:
         pieces = fetched
-    far_out, beside, in_sum = after(far_out, beside if on_line else in_sum, in_sum)
+    chunk = table()
+    activations, out_grads, in_sum = after(activations, out_grads, in_sum)
+    cut = [
+        [
+            lax.dynamic_slice_in_dim(array, chunk[place] * width, width, 1)
+            for place in places
+        ]
+        for array, places in (
+            (out_grads, far_own),
+            (activations, far_other),
+            (out_grads, far_other + [1]),
+        )
+    ]
+    far_out, in_sum, cut = after(far_out, in_sum, cut)
+    grads_own, acts_other, grads_other = cut
+    if on_line:
+        far_out, beside = after(far_out, beside)
+        pieces = [queries, beside, beside_other]
     others_out = [to_core(a) for a in far_out] + [other_out]
-    if on_line:
-        pieces = [queries, beside, beside_other]
-    (out_sum,) = project([(out_grads, far_out, far_own)], table, [out_sum])
+    out_sum = add_chunks(out_sum, grads_own, far_out)
     if on_line:
         across, out_sum = after(across, out_sum)
         across_other = to_core(across)
     f_stack, scores = gradients(
         table,
-        (activations, others_in, far_other),
-        (out_grads, others_out, far_other + [1]),
+        (acts_other, others_in),
+        (grads_other, others_out),
         (in_sum, out_sum),
         segments,
         loss_mask,

time: 23.4 us -> 21.9 us (0.936)
  Pallas kernels: 8.71 us -> 6.49 us
  local copies, waits for them, and re-layouts: 1.91 us -> 3.28 us
  waiting for transfers between devices: 2.11 us -> 1.53 us
    pallas_call x1, Pallas kernels: 2.94 us -> 1.62 us  [gradients(): pl.pallas_call(kernel, out_shape=(jax.ShapeDtypeStruct((2 * TRAJ_DEV, fla...]
    pallas_call x3 -> x2, Pallas kernels: 4.86 us -> 3.67 us  [project(): pl.pallas_call(kernel, out_shape=shapes, in_specs=[ANY] * n + [VMEM] * (t...]
    dynamic_slice x0 -> x1, local copies, waits for them, and re-layouts: none -> 1.18 us  [body(): lax.dynamic_slice_in_dim(array, chunk[place] * width, width, 1)]
    ppermute x2, waiting for transfers between devices: 0.62 us -> 0.01 us  [from_chip(): return lax.ppermute(a, 'fsdp', [((i + d) % chips, i) for i in range(chips)])]
    pallas_call x0 -> x1, Pallas kernels: none -> 0.29 us  [add_chunks(): pl.pallas_call(kernel, out_shape=jax.ShapeDtypeStruct(base.shape, base.dt...]
    unnamed x10 -> x12, local copies, waits for them, and re-layouts: 1.91 us -> 2.1 us
  transfers between devices with their start and end apart: 10 -> 10, of which waited for: 2 -> 1; matrix products, arithmetic and copies ran while one was open for 0% -> 5% of each run, Pallas kernels for 34% -> 26%
where the time goes in v4:
time: 21.9 us; the launch traced here: 21.6 us
  starting transfers between devices  10.1 us (46%)
  Pallas kernels  6.49 us (30%)
  local copies, waits for them, and re-layouts  3.28 us (15%)
  waiting for transfers between devices  1.53 us (7%)
    pallas_call x2, Pallas kernels, project(): pl.pallas_call(kernel, out_shape=shapes, in_specs=[ANY] * n + [VMEM] * (t...  3.67 us
    ppermute x1, starting transfers between devices, fetch_queries(): lax.ppermute(queries, ('traj', 'sub'), [(2 * ((z + 1) % n), 2 * z) for z...  3.6 us
    ppermute x2, starting transfers between devices, from_chip(): return lax.ppermute(a, 'fsdp', [((i + d) % chips, i) for i in range(chips)])  3.09 us
    unnamed x12, local copies, waits for them, and re-layouts  2.1 us
    ppermute x1, starting transfers between devices, fetch_queries(): lax.ppermute(queries, ('traj', 'sub'), [(2 * ((z + 2) % n), 2 * z) for z...  1.91 us
    pallas_call x1, Pallas kernels, gradients(): pl.pallas_call(kernel, out_shape=(jax.ShapeDtypeStruct((2 * TRAJ_DEV, fla...  1.62 us
    ppermute x6, starting transfers between devices, to_core(): return lax.ppermute(a, 'sub', [(0, 1), (1, 0)])  1.53 us
    ppermute x1, waiting for transfers between devices, fetch_queries(): lax.ppermute(queries, ('traj', 'sub'), [(2 * ((z + 2) % n), 2 * z) for z...  1.49 us
  transfers between devices with their start and end apart: 10, of which 1 were waited for; matrix products, arithmetic and copies ran while one was open for 5% of the time, Pallas kernels for 26%

profile of v4, /device:TPU:0, one launch (start us, length us, event | category | flops | bytes accessed | tf_op | source)
XLA Modules:
  0.0 21.6 jit_solution(13040076609681152353)
XLA Ops:
  0.0 0.5 %collective-permute-start.3 = (bf16[64,2048]{1,0:T(8,128)(2,1)}, bf16[64,2048]{1,0:T(8,128)(2,1)S(1)}, u32[]{:S(2)}, u32[]{:S(2)}) collective-permute-start(bf16[64,2048]{1,0:T(8,128)(2,1)} %refs_2_.1), channel_id=1, source_target_pairs={{0,1},{1,0},{2,3},{3,2},{4,5},{5,4},{6,7},{7,6},{8,9},{9,8},{10,11... | collective-permute-start | bytes 786440 | tf_op jit(solution)/shard_map/ppermute | solution.py:222
  0.5 2.5 %collective-permute-start.2 = (bf16[64,2048]{1,0:T(8,128)(2,1)}, bf16[64,2048]{1,0:T(8,128)(2,1)S(1)}, u32[]{:S(2)}, u32[]{:S(2)}) collective-permute-start(bf16[64,2048]{1,0:T(8,128)(2,1)} %refs_2_.1), channel_id=1, source_target_pairs={{2,0},{0,2},{3,1},{1,3},{6,4},{4,6},{7,5},{5,7},{10,8},{8,10},{11,... | collective-permute-start | bytes 786440 | tf_op jit(solution)/shard_map/ppermute | solution.py:225
  2.9 3.6 %collective-permute-start.1 = (f32[16,4096]{1,0:T(8,128)}, f32[16,4096]{1,0:T(8,128)S(1)}, u32[]{:S(2)}, u32[]{:S(2)}) collective-permute-start(f32[16,4096]{1,0:T(8,128)} %refs_6_.1), channel_id=1, source_target_pairs={{4,0},{8,4},{12,8},{0,12},{13,1},{1,5},{5,9},{9,13},{6,2},{10,6},{... | collective-permute-start | bytes 786440 | tf_op jit(solution)/shard_map/ppermute | solution.py:208
  6.5 1.9 %collective-permute-start.8 = (f32[16,4096]{1,0:T(8,128)}, f32[16,4096]{1,0:T(8,128)S(1)}, u32[]{:S(2)}, u32[]{:S(2)}) collective-permute-start(f32[16,4096]{1,0:T(8,128)} %refs_6_.1), channel_id=1, source_target_pairs={{8,0},{12,4},{0,8},{4,12},{10,2},{14,6},{2,10},{6,14},{24,16},{28,... | collective-permute-start | bytes 786440 | tf_op jit(solution)/shard_map/ppermute | solution.py:214
  8.5 0.6 %collective-permute-start = (bf16[64,2048]{1,0:T(8,128)(2,1)}, bf16[64,2048]{1,0:T(8,128)(2,1)S(1)}, u32[]{:S(2)}, u32[]{:S(2)}) collective-permute-start(bf16[64,2048]{1,0:T(8,128)(2,1)} %refs_4_.1), channel_id=1, source_target_pairs={{2,0},{0,2},{3,1},{1,3},{6,4},{4,6},{7,5},{5,7},{10,8},{8,10},{11,... | collective-permute-start | bytes 786440 | tf_op jit(solution)/shard_map/ppermute | solution.py:225
  9.1 0.0 collective-permute-done.3.refs_3_
  9.1 0.9 %copy-done = bf16[64,2048]{1,0:T(8,128)(2,1)S(1)} copy-done((bf16[64,2048]{1,0:T(8,128)(2,1)S(1)}, bf16[64,2048]{1,0:T(8,128)(2,1)}, u32[]{:S(2)}) %copy-start) | copy-done | bytes 262168
  10.0 0.9 %copy-done.1 = bf16[64,2048]{1,0:T(8,128)(2,1)S(1)} copy-done((bf16[64,2048]{1,0:T(8,128)(2,1)S(1)}, bf16[64,2048]{1,0:T(8,128)(2,1)}, u32[]{:S(2)}) %copy-start.1) | copy-done | bytes 262168
  11.0 2.2 %shard_map.73 = (f32[128,64]{1,0:T(8,128)S(1)}, f32[128,64]{1,0:T(8,128)S(1)}) custom-call(bf16[128,8192]{1,0:T(8,128)(2,1)} %refs_0_.3, bf16[128,8192]{1,0:T(8,128)(2,1)} %refs_1_.1, bf16[64,2048]{1,0:T(8,128)(2,1)S(1)} %copy-done, bf16[64,2048]{1,0:T(8,128)(2,1)S(1)} %collective-permute-done.3.refs_3_, bf16[64,2048]{1,0:T(8,128)(2,1)S(1)} %copy-done.1), custom_call_target="tpu_custom_call" | custom-call | flops 1 | bytes 1 | tf_op jit(solution)/shard_map/pallas_call | solution.py:74
  13.1 0.0 copy-start.5
  13.2 0.0 collective-permute-done.2.refs_1_
  13.2 1.5 %shard_map.74.refs_9_ = f32[128,64]{1,0:T(8,128)S(1)} custom-call(bf16[128,8192]{1,0:T(8,128)(2,1)} %refs_0_.3, bf16[64,2048]{1,0:T(8,128)(2,1)S(1)} %collective-permute-done.2.refs_1_, f32[128,64]{1,0:T(8,128)S(1)} %get-tuple-element.31.refs_2_), custom_call_target="tpu_custom_call" | custom-call | flops 1 | bytes 1 | tf_op jit(solution)/shard_map/pallas_call | solution.py:74
  14.7 0.0 copy-start.2
  14.7 0.0 copy-start.3
  14.7 0.0 copy-start.4
  14.7 0.2 copy-done.5
  14.9 1.2 %constant_dynamic-slice_fusion = (bf16[128,2048]{1,0:T(8,128)(2,1)S(1)}, bf16[128,2048]{1,0:T(8,128)(2,1)S(1)}, bf16[128,2048]{1,0:T(8,128)(2,1)S(1)}, bf16[128,2048]{1,0:T(8,128)(2,1)S(1)}) fusion(bf16[128,8192]{1,0:T(8,128)(2,1)S(1)} %copy-done.5, s32[]{:T(128)S(6)} %select_n.12, s32[]{:T(128)S(6)} %select_n.11, s32[]{:T(128)S(6)} %select_n.10, ...), kind=kLoop, calls=%fused_computation | loop fusion | bytes 4194316 | tf_op jit(solution)/shard_map/dynamic_slice | solution.py:266
  16.1 0.0 collective-permute-done.refs_1_
  16.1 0.1 collective-permute-start.7
  16.2 0.5 %collective-permute-start.5 = (bf16[64,2048]{1,0:T(8,128)(2,1)S(1)}, bf16[64,2048]{1,0:T(8,128)(2,1)S(1)}, u32[]{:S(2)}, u32[]{:S(2)}) collective-permute-start(bf16[64,2048]{1,0:T(8,128)(2,1)S(1)} %collective-permute-done.refs_1_), channel_id=1, source_target_pairs={{0,1},{1,0},{2,3},{3,2},{4,5},{5,4},{6,7},{7,6},{8,9},{9,8},{10,11... | collective-permute-start | bytes 786440 | tf_op jit(solution)/shard_map/ppermute | solution.py:222
  16.7 0.1 collective-permute-start.4
  16.7 0.4 %collective-permute-start.6 = (bf16[64,2048]{1,0:T(8,128)(2,1)S(1)}, bf16[64,2048]{1,0:T(8,128)(2,1)S(1)}, u32[]{:S(2)}, u32[]{:S(2)}) collective-permute-start(bf16[64,2048]{1,0:T(8,128)(2,1)S(1)} %copy-done.1), channel_id=1, source_target_pairs={{0,1},{1,0},{2,3},{3,2},{4,5},{5,4},{6,7},{7,6},{8,9},{9,8},{10,11... | collective-permute-start | bytes 786440 | tf_op jit(solution)/shard_map/ppermute | solution.py:222
  17.2 0.3 %shard_map.75.refs_10_ = f32[128,64]{1,0:T(8,128)S(1)} custom-call(f32[128,64]{1,0:T(8,128)S(1)} %get-tuple-element.45.base_ref, bf16[128,2048]{1,0:T(8,128)(2,1)S(1)} %get-tuple-element.46.refs_0_, bf16[64,2048]{1,0:T(8,128)(2,1)S(1)} %collective-permute-done.refs_1_), custom_call_target="tpu_custom_call" | custom-call | flops 1 | bytes 1 | tf_op jit(solution)/shard_map/pallas_call | solution.py:94
  17.5 1.5 %collective-permute-done.8.here_ref = f32[16,4096]{1,0:T(8,128)S(1)} collective-permute-done((f32[16,4096]{1,0:T(8,128)}, f32[16,4096]{1,0:T(8,128)S(1)}, u32[]{:S(2)}, u32[]{:S(2)}) %collective-permute-start.8) | collective-permute-done | bytes 262176 | tf_op jit(solution)/shard_map/ppermute | solution.py:214
  19.0 0.0 collective-permute-start.9
  19.0 0.0 collective-permute-done.5.refs_4_
  19.0 0.0 collective-permute-done.7.refs_8_
  19.0 0.0 collective-permute-done.4.refs_3_
  19.0 0.0 collective-permute-done.6.refs_5_
  19.0 1.6 %shard_map.76 = (bf16[16,4096]{1,0:T(8,128)(2,1)S(1)}, f32[8,64]{1,0:T(8,128)S(1)}) custom-call(bf16[128,2048]{1,0:T(8,128)(2,1)S(1)} %get-tuple-element.36.refs_0_, bf16[128,2048]{1,0:T(8,128)(2,1)S(1)} %get-tuple-element.37.refs_1_, bf16[128,2048]{1,0:T(8,128)(2,1)S(1)} %get-tuple-element.38.refs_2_, bf16[64,2048]{1,0:T(8,128)(2,1)S(1)} %collective-permute-done.4.refs_3_, ...), custom_call_target="tpu_custom_call" | custom-call | flops 1 | bytes 1 | tf_op jit(solution)/shard_map/pallas_call | solution.py:158
  20.7 0.0 collective-permute-done.9.there_ref
  20.7 0.9 %shard_map.77 = f32[8,64]{1,0:T(8,128)} custom-call(f32[8,64]{1,0:T(8,128)S(1)} %get-tuple-element.48.base_ref, bf16[16,4096]{1,0:T(8,128)(2,1)S(1)} %get-tuple-element.49.stack_ref, f32[16,4096]{1,0:T(8,128)S(1)} %collective-permute-done.8.here_ref, f32[16,4096]{1,0:T(8,128)S(1)} %collective-permute-done.9.there_ref), custom_call_target="tpu_custom_call" | custom-call | flops 1 | bytes 1 | tf_op jit(solution)/shard_map/pallas_call | solution.py:189
  (6 shorter events, 0.0 us)
Async XLA Ops:
  0.0 9.1 %collective-permute-start.3 = (bf16[64,2048]{1,0:T(8,128)(2,1)}, bf16[64,2048]{1,0:T(8,128)(2,1)S(1)}, u32[]{:S(2)}, u32[]{:S(2)}) collective-permute-start(bf16[64,2048]{1,0:T(8,128)(2,1)} %refs_2_.1), channel_id=1, source_target_pairs={{0,1},{1,0},{2,3},{3,2},{4,5},{5,4},{6,7},{7,6},{8,9},{9,8},{10,11... | collective-permute-start | bytes 786440 | tf_op jit(solution)/shard_map/ppermute | solution.py:222
  0.5 12.7 %collective-permute-start.2 = (bf16[64,2048]{1,0:T(8,128)(2,1)}, bf16[64,2048]{1,0:T(8,128)(2,1)S(1)}, u32[]{:S(2)}, u32[]{:S(2)}) collective-permute-start(bf16[64,2048]{1,0:T(8,128)(2,1)} %refs_2_.1), channel_id=1, source_target_pairs={{2,0},{0,2},{3,1},{1,3},{6,4},{4,6},{7,5},{5,7},{10,8},{8,10},{11,... | collective-permute-start | bytes 786440 | tf_op jit(solution)/shard_map/ppermute | solution.py:225
  2.9 11.8 %collective-permute-start.1 = (f32[16,4096]{1,0:T(8,128)}, f32[16,4096]{1,0:T(8,128)S(1)}, u32[]{:S(2)}, u32[]{:S(2)}) collective-permute-start(f32[16,4096]{1,0:T(8,128)} %refs_6_.1), channel_id=1, source_target_pairs={{4,0},{8,4},{12,8},{0,12},{13,1},{1,5},{5,9},{9,13},{6,2},{10,6},{... | collective-permute-start | bytes 786440 | tf_op jit(solution)/shard_map/ppermute | solution.py:208
  6.5 12.4 %collective-permute-start.8 = (f32[16,4096]{1,0:T(8,128)}, f32[16,4096]{1,0:T(8,128)S(1)}, u32[]{:S(2)}, u32[]{:S(2)}) collective-permute-start(f32[16,4096]{1,0:T(8,128)} %refs_6_.1), channel_id=1, source_target_pairs={{8,0},{12,4},{0,8},{4,12},{10,2},{14,6},{2,10},{6,14},{24,16},{28,... | collective-permute-start | bytes 786440 | tf_op jit(solution)/shard_map/ppermute | solution.py:214
  8.5 7.6 %collective-permute-start = (bf16[64,2048]{1,0:T(8,128)(2,1)}, bf16[64,2048]{1,0:T(8,128)(2,1)S(1)}, u32[]{:S(2)}, u32[]{:S(2)}) collective-permute-start(bf16[64,2048]{1,0:T(8,128)(2,1)} %refs_4_.1), channel_id=1, source_target_pairs={{2,0},{0,2},{3,1},{1,3},{6,4},{4,6},{7,5},{5,7},{10,8},{8,10},{11,... | collective-permute-start | bytes 786440 | tf_op jit(solution)/shard_map/ppermute | solution.py:225
  9.1 1.0 %copy-start = (bf16[64,2048]{1,0:T(8,128)(2,1)S(1)}, bf16[64,2048]{1,0:T(8,128)(2,1)}, u32[]{:S(2)}) copy-start(bf16[64,2048]{1,0:T(8,128)(2,1)} %refs_2_.1) | copy-start | bytes 786436
  10.0 0.9 %copy-start.1 = (bf16[64,2048]{1,0:T(8,128)(2,1)S(1)}, bf16[64,2048]{1,0:T(8,128)(2,1)}, u32[]{:S(2)}) copy-start(bf16[64,2048]{1,0:T(8,128)(2,1)} %refs_4_.1) | copy-start | bytes 786436
  13.1 1.8 %copy-start.5 = (bf16[128,8192]{1,0:T(8,128)(2,1)S(1)}, bf16[128,8192]{1,0:T(8,128)(2,1)}, u32[]{:S(2)}) copy-start(bf16[128,8192]{1,0:T(8,128)(2,1)} %refs_1_.1) | copy-start | bytes 6291460
  14.7 4.3 %copy-start.2 = (f32[16,4096]{1,0:T(8,128)S(1)}, f32[16,4096]{1,0:T(8,128)}, u32[]{:S(2)}) copy-start(f32[16,4096]{1,0:T(8,128)} %refs_6_.1) | copy-start | bytes 786436
  14.7 4.3 %copy-start.3 = (s32[1,128]{1,0:T(1,128)S(1)}, s32[1,128]{1,0:T(1,128)}, u32[]{:S(2)}) copy-start(s32[1,128]{1,0:T(1,128)} %refs_11_.1) | copy-start | bytes 1540
  14.7 4.3 %copy-start.4 = (s32[1,128]{1,0:T(1,128)S(1)}, s32[1,128]{1,0:T(1,128)}, u32[]{:S(2)}) copy-start(s32[1,128]{1,0:T(1,128)} %refs_12_.1) | copy-start | bytes 1540
  16.1 2.9 %collective-permute-start.7 = (f32[16,4096]{1,0:T(8,128)S(1)}, f32[16,4096]{1,0:T(8,128)S(1)}, u32[]{:S(2)}, u32[]{:S(2)}) collective-permute-start(f32[16,4096]{1,0:T(8,128)S(1)} %collective-permute-done.1.refs_7_), channel_id=1, source_target_pairs={{0,1},{1,0},{2,3},{3,2},{4,5},{5,4},{6,7},{7,6},{8,9},{9,8},{10,11... | collective-permute-start | bytes 786440 | tf_op jit(solution)/shard_map/ppermute | solution.py:222
  16.2 2.8 %collective-permute-start.5 = (bf16[64,2048]{1,0:T(8,128)(2,1)S(1)}, bf16[64,2048]{1,0:T(8,128)(2,1)S(1)}, u32[]{:S(2)}, u32[]{:S(2)}) collective-permute-start(bf16[64,2048]{1,0:T(8,128)(2,1)S(1)} %collective-permute-done.refs_1_), channel_id=1, source_target_pairs={{0,1},{1,0},{2,3},{3,2},{4,5},{5,4},{6,7},{7,6},{8,9},{9,8},{10,11... | collective-permute-start | bytes 786440 | tf_op jit(solution)/shard_map/ppermute | solution.py:222
  16.7 2.3 %collective-permute-start.4 = (bf16[64,2048]{1,0:T(8,128)(2,1)S(1)}, bf16[64,2048]{1,0:T(8,128)(2,1)S(1)}, u32[]{:S(2)}, u32[]{:S(2)}) collective-permute-start(bf16[64,2048]{1,0:T(8,128)(2,1)S(1)} %collective-permute-done.2.refs_1_), channel_id=1, source_target_pairs={{0,1},{1,0},{2,3},{3,2},{4,5},{5,4},{6,7},{7,6},{8,9},{9,8},{10,11... | collective-permute-start | bytes 786440 | tf_op jit(solution)/shard_map/ppermute | solution.py:222
  16.7 2.2 %collective-permute-start.6 = (bf16[64,2048]{1,0:T(8,128)(2,1)S(1)}, bf16[64,2048]{1,0:T(8,128)(2,1)S(1)}, u32[]{:S(2)}, u32[]{:S(2)}) collective-permute-start(bf16[64,2048]{1,0:T(8,128)(2,1)S(1)} %copy-done.1), channel_id=1, source_target_pairs={{0,1},{1,0},{2,3},{3,2},{4,5},{5,4},{6,7},{7,6},{8,9},{9,8},{10,11... | collective-permute-start | bytes 786440 | tf_op jit(solution)/shard_map/ppermute | solution.py:222
  19.0 1.7 %collective-permute-start.9 = (f32[16,4096]{1,0:T(8,128)S(1)}, f32[16,4096]{1,0:T(8,128)S(1)}, u32[]{:S(2)}, u32[]{:S(2)}) collective-permute-start(f32[16,4096]{1,0:T(8,128)S(1)} %collective-permute-done.8.here_ref), channel_id=1, source_target_pairs={{0,1},{1,0},{2,3},{3,2},{4,5},{5,4},{6,7},{7,6},{8,9},{9,8},{10,11... | collective-permute-start | bytes 786440 | tf_op jit(solution)/shard_map/ppermute | solution.py:222

commit v5 on v4

--- a/solution.py
+++ b/solution.py
@@ -245,17 +245,20 @@
         return chunks + [lax.rem(b, 4) for b in blocks] + [core]
 
     in_sum, out_sum = project(
-        [(activations, [proj_in, to_core(proj_in)], [0, 1]), (out_grads, [proj_out], [0])],
+        [(activations, [proj_in], [0]), (out_grads, [proj_out], [0])],
         table,
         [],
     )
-    far_in, late_out, in_sum, out_sum = after(far_in, proj_out, in_sum, out_sum)
+    first = fetched[:1] if on_line else []
+    far_in, first, late_out, in_sum, out_sum = after(far_in, first, proj_out, in_sum, out_sum)
+    fetched = first + fetched[len(first) :]
     others_in = [to_core(a) for a in far_in]
     other_out = to_core(late_out)
-    (in_sum,) = project([(activations, far_in, far_own)], table, [in_sum])
+    (in_sum,) = project(
+        [(activations, far_in + [to_core(proj_in)], far_own + [1])], table, [in_sum]
+    )
     if on_line:
         beside, across = fetched
-        beside, in_sum = after(beside, in_sum)
         beside_other = to_core(beside)
     else:
         pieces = fetched

time: 21.9 us -> 21.5 us (0.982)
  waiting for transfers between devices: 1.53 us -> 1.13 us
    ppermute x1, waiting for transfers between devices: 1.49 us -> 0.79 us  [fetch_queries(): lax.ppermute(queries, ('traj', 'sub'), [(2 * ((z + 2) % n), 2 * z) for z...]
    ppermute x6, starting transfers between devices: 1.53 us -> 1.01 us  [to_core(): return lax.ppermute(a, 'sub', [(0, 1), (1, 0)])]
    ppermute x2, starting transfers between devices: 3.09 us -> 3.54 us  [from_chip(): return lax.ppermute(a, 'fsdp', [((i + d) % chips, i) for i in range(chips)])]
    ppermute x6, waiting for transfers between devices: 0.03 us -> 0.33 us  [to_core(): return lax.ppermute(a, 'sub', [(0, 1), (1, 0)])]
    unnamed x12 -> x14, local copies, waits for them, and re-layouts: 2.1 us -> 1.93 us
  transfers between devices with their start and end apart: 10 -> 10, of which waited for: 1 -> 2; matrix products, arithmetic and copies ran while one was open for 5% -> 6% of each run, Pallas kernels for 26% -> 27%
where the time goes in v5:
time: 21.5 us; the launch traced here: 21.3 us
  starting transfers between devices  10.1 us (47%)
  Pallas kernels  6.68 us (31%)
  local copies, waits for them, and re-layouts  3.24 us (15%)
  waiting for transfers between devices  1.13 us (5%)
    pallas_call x2, Pallas kernels, project(): pl.pallas_call(kernel, out_shape=shapes, in_specs=[ANY] * n + [VMEM] * (t...  3.86 us
    ppermute x1, starting transfers between devices, fetch_queries(): lax.ppermute(queries, ('traj', 'sub'), [(2 * ((z + 1) % n), 2 * z) for z...  3.6 us
    ppermute x2, starting transfers between devices, from_chip(): return lax.ppermute(a, 'fsdp', [((i + d) % chips, i) for i in range(chips)])  3.54 us
    unnamed x14, local copies, waits for them, and re-layouts  1.93 us
    ppermute x1, starting transfers between devices, fetch_queries(): lax.ppermute(queries, ('traj', 'sub'), [(2 * ((z + 2) % n), 2 * z) for z...  1.91 us
    pallas_call x1, Pallas kernels, gradients(): pl.pallas_call(kernel, out_shape=(jax.ShapeDtypeStruct((2 * TRAJ_DEV, fla...  1.62 us
    dynamic_slice x1, local copies, waits for them, and re-layouts, body(): lax.dynamic_slice_in_dim(array, chunk[place] * width, width, 1)  1.31 us
    ppermute x6, starting transfers between devices, to_core(): return lax.ppermute(a, 'sub', [(0, 1), (1, 0)])  1.01 us
  transfers between devices with their start and end apart: 10, of which 2 were waited for; matrix products, arithmetic and copies ran while one was open for 6% of the time, Pallas kernels for 27%

profile of v5, /device:TPU:0, one launch (start us, length us, event | category | flops | bytes accessed | tf_op | source)
XLA Modules:
  0.0 21.3 jit_solution(14226113225121642432)
XLA Ops:
  0.0 2.9 %collective-permute-start.1 = (bf16[64,2048]{1,0:T(8,128)(2,1)}, bf16[64,2048]{1,0:T(8,128)(2,1)S(1)}, u32[]{:S(2)}, u32[]{:S(2)}) collective-permute-start(bf16[64,2048]{1,0:T(8,128)(2,1)} %refs_2_.1), channel_id=1, source_target_pairs={{2,0},{0,2},{3,1},{1,3},{6,4},{4,6},{7,5},{5,7},{10,8},{8,10},{11,... | collective-permute-start | bytes 786440 | tf_op jit(solution)/shard_map/ppermute | solution.py:225
  2.9 3.6 %collective-permute-start.2 = (f32[16,4096]{1,0:T(8,128)}, f32[16,4096]{1,0:T(8,128)S(1)}, u32[]{:S(2)}, u32[]{:S(2)}) collective-permute-start(f32[16,4096]{1,0:T(8,128)} %refs_6_.1), channel_id=1, source_target_pairs={{4,0},{8,4},{12,8},{0,12},{13,1},{1,5},{5,9},{9,13},{6,2},{10,6},{... | collective-permute-start | bytes 786440 | tf_op jit(solution)/shard_map/ppermute | solution.py:208
  6.5 0.0 collective-permute-start.3
  6.5 1.9 %collective-permute-start.8 = (f32[16,4096]{1,0:T(8,128)}, f32[16,4096]{1,0:T(8,128)S(1)}, u32[]{:S(2)}, u32[]{:S(2)}) collective-permute-start(f32[16,4096]{1,0:T(8,128)} %refs_6_.1), channel_id=1, source_target_pairs={{8,0},{12,4},{0,8},{4,12},{10,2},{14,6},{2,10},{6,14},{24,16},{28,... | collective-permute-start | bytes 786440 | tf_op jit(solution)/shard_map/ppermute | solution.py:214
  8.5 0.6 %collective-permute-start = (bf16[64,2048]{1,0:T(8,128)(2,1)}, bf16[64,2048]{1,0:T(8,128)(2,1)S(1)}, u32[]{:S(2)}, u32[]{:S(2)}) collective-permute-start(bf16[64,2048]{1,0:T(8,128)(2,1)} %refs_3_.1), channel_id=1, source_target_pairs={{2,0},{0,2},{3,1},{1,3},{6,4},{4,6},{7,5},{5,7},{10,8},{8,10},{11,... | collective-permute-start | bytes 786440 | tf_op jit(solution)/shard_map/ppermute | solution.py:225
  9.1 0.9 %copy-done = bf16[64,2048]{1,0:T(8,128)(2,1)S(1)} copy-done((bf16[64,2048]{1,0:T(8,128)(2,1)S(1)}, bf16[64,2048]{1,0:T(8,128)(2,1)}, u32[]{:S(2)}) %copy-start) | copy-done | bytes 262168
  10.0 0.9 %copy-done.1 = bf16[64,2048]{1,0:T(8,128)(2,1)S(1)} copy-done((bf16[64,2048]{1,0:T(8,128)(2,1)S(1)}, bf16[64,2048]{1,0:T(8,128)(2,1)}, u32[]{:S(2)}) %copy-start.1) | copy-done | bytes 262168
  11.0 1.9 %shard_map.73 = (f32[128,64]{1,0:T(8,128)S(1)}, f32[128,64]{1,0:T(8,128)S(1)}) custom-call(bf16[128,8192]{1,0:T(8,128)(2,1)} %refs_0_.3, bf16[128,8192]{1,0:T(8,128)(2,1)} %refs_1_.1, bf16[64,2048]{1,0:T(8,128)(2,1)S(1)} %copy-done, bf16[64,2048]{1,0:T(8,128)(2,1)S(1)} %copy-done.1), custom_call_target="tpu_custom_call" | custom-call | flops 1 | bytes 1 | tf_op jit(solution)/shard_map/pallas_call | solution.py:74
  12.8 0.0 copy-start.6
  12.9 0.0 collective-permute-done.1.refs_1_
  12.9 0.0 collective-permute-done.2.refs_7_
  12.9 0.1 collective-permute-start.4
  13.0 0.0 collective-permute-done.3.refs_2_
  13.0 2.0 %shard_map.74.refs_9_ = f32[128,64]{1,0:T(8,128)S(1)} custom-call(bf16[128,8192]{1,0:T(8,128)(2,1)} %refs_0_.3, bf16[64,2048]{1,0:T(8,128)(2,1)S(1)} %collective-permute-done.1.refs_1_, bf16[64,2048]{1,0:T(8,128)(2,1)S(1)} %collective-permute-done.3.refs_2_, f32[128,64]{1,0:T(8,128)S(1)} %get-tuple-element.30.refs_3_), custom_call_target="tpu_custom_call" | custom-call | flops 1 | bytes 1 | tf_op jit(solution)/shard_map/pallas_call | solution.py:74
  15.0 0.0 copy-start.2
  15.0 0.0 copy-start.3
  15.0 0.0 copy-start.4
  15.0 0.0 copy-start.5
  15.0 1.3 %constant_dynamic-slice_fusion = (bf16[128,2048]{1,0:T(8,128)(2,1)S(1)}, bf16[128,2048]{1,0:T(8,128)(2,1)S(1)}, bf16[128,2048]{1,0:T(8,128)(2,1)S(1)}, bf16[128,2048]{1,0:T(8,128)(2,1)S(1)}) fusion(bf16[128,8192]{1,0:T(8,128)(2,1)S(1)} %copy-done.6, s32[]{:T(128)S(6)} %select_n.12, s32[]{:T(128)S(6)} %select_n.11, s32[]{:T(128)S(6)} %select_n.10, ...), kind=kLoop, calls=%fused_computation | loop fusion | bytes 4194316 | tf_op jit(solution)/shard_map/dynamic_slice | solution.py:269
  16.4 0.0 collective-permute-done.refs_1_
  16.4 0.4 %collective-permute-start.5 = (bf16[64,2048]{1,0:T(8,128)(2,1)S(1)}, bf16[64,2048]{1,0:T(8,128)(2,1)S(1)}, u32[]{:S(2)}, u32[]{:S(2)}) collective-permute-start(bf16[64,2048]{1,0:T(8,128)(2,1)S(1)} %collective-permute-done.refs_1_), channel_id=1, source_target_pairs={{0,1},{1,0},{2,3},{3,2},{4,5},{5,4},{6,7},{7,6},{8,9},{9,8},{10,11... | collective-permute-start | bytes 786440 | tf_op jit(solution)/shard_map/ppermute | solution.py:222
  16.8 0.2 collective-permute-start.7
  17.0 0.4 %collective-permute-start.6 = (bf16[64,2048]{1,0:T(8,128)(2,1)S(1)}, bf16[64,2048]{1,0:T(8,128)(2,1)S(1)}, u32[]{:S(2)}, u32[]{:S(2)}) collective-permute-start(bf16[64,2048]{1,0:T(8,128)(2,1)S(1)} %copy-done.2), channel_id=1, source_target_pairs={{0,1},{1,0},{2,3},{3,2},{4,5},{5,4},{6,7},{7,6},{8,9},{9,8},{10,11... | collective-permute-start | bytes 786440 | tf_op jit(solution)/shard_map/ppermute | solution.py:222
  17.3 0.3 %shard_map.75.refs_10_ = f32[128,64]{1,0:T(8,128)S(1)} custom-call(f32[128,64]{1,0:T(8,128)S(1)} %get-tuple-element.43.base_ref, bf16[128,2048]{1,0:T(8,128)(2,1)S(1)} %get-tuple-element.44.refs_0_, bf16[64,2048]{1,0:T(8,128)(2,1)S(1)} %collective-permute-done.refs_1_), custom_call_target="tpu_custom_call" | custom-call | flops 1 | bytes 1 | tf_op jit(solution)/shard_map/pallas_call | solution.py:94
  17.6 0.8 %collective-permute-done.8.here_ref = f32[16,4096]{1,0:T(8,128)S(1)} collective-permute-done((f32[16,4096]{1,0:T(8,128)}, f32[16,4096]{1,0:T(8,128)S(1)}, u32[]{:S(2)}, u32[]{:S(2)}) %collective-permute-start.8) | collective-permute-done | bytes 262176 | tf_op jit(solution)/shard_map/ppermute | solution.py:214
  18.4 0.0 collective-permute-start.9
  18.4 0.0 collective-permute-done.5.refs_4_
  18.4 0.0 collective-permute-done.4.refs_3_
  18.4 0.3 %collective-permute-done.6.refs_5_ = bf16[64,2048]{1,0:T(8,128)(2,1)S(1)} collective-permute-done((bf16[64,2048]{1,0:T(8,128)(2,1)S(1)}, bf16[64,2048]{1,0:T(8,128)(2,1)S(1)}, u32[]{:S(2)}, u32[]{:S(2)}) %collective-permute-start.6) | collective-permute-done | bytes 262176 | tf_op jit(solution)/shard_map/ppermute | solution.py:222
  18.7 1.6 %shard_map.76 = (bf16[16,4096]{1,0:T(8,128)(2,1)S(1)}, f32[8,64]{1,0:T(8,128)S(1)}) custom-call(bf16[128,2048]{1,0:T(8,128)(2,1)S(1)} %get-tuple-element.34.refs_0_, bf16[128,2048]{1,0:T(8,128)(2,1)S(1)} %get-tuple-element.35.refs_1_, bf16[128,2048]{1,0:T(8,128)(2,1)S(1)} %get-tuple-element.36.refs_2_, bf16[64,2048]{1,0:T(8,128)(2,1)S(1)} %collective-permute-done.4.refs_3_, ...), custom_call_target="tpu_custom_call" | custom-call | flops 1 | bytes 1 | tf_op jit(solution)/shard_map/pallas_call | solution.py:158
  20.4 0.0 collective-permute-done.9.there_ref
  20.4 0.9 %shard_map.77 = f32[8,64]{1,0:T(8,128)} custom-call(f32[8,64]{1,0:T(8,128)S(1)} %get-tuple-element.46.base_ref, bf16[16,4096]{1,0:T(8,128)(2,1)S(1)} %get-tuple-element.47.stack_ref, f32[16,4096]{1,0:T(8,128)S(1)} %collective-permute-done.8.here_ref, f32[16,4096]{1,0:T(8,128)S(1)} %collective-permute-done.9.there_ref), custom_call_target="tpu_custom_call" | custom-call | flops 1 | bytes 1 | tf_op jit(solution)/shard_map/pallas_call | solution.py:189
  (8 shorter events, 0.0 us)
Async XLA Ops:
  0.0 12.9 %collective-permute-start.1 = (bf16[64,2048]{1,0:T(8,128)(2,1)}, bf16[64,2048]{1,0:T(8,128)(2,1)S(1)}, u32[]{:S(2)}, u32[]{:S(2)}) collective-permute-start(bf16[64,2048]{1,0:T(8,128)(2,1)} %refs_2_.1), channel_id=1, source_target_pairs={{2,0},{0,2},{3,1},{1,3},{6,4},{4,6},{7,5},{5,7},{10,8},{8,10},{11,... | collective-permute-start | bytes 786440 | tf_op jit(solution)/shard_map/ppermute | solution.py:225
  2.9 9.9 %collective-permute-start.2 = (f32[16,4096]{1,0:T(8,128)}, f32[16,4096]{1,0:T(8,128)S(1)}, u32[]{:S(2)}, u32[]{:S(2)}) collective-permute-start(f32[16,4096]{1,0:T(8,128)} %refs_6_.1), channel_id=1, source_target_pairs={{4,0},{8,4},{12,8},{0,12},{13,1},{1,5},{5,9},{9,13},{6,2},{10,6},{... | collective-permute-start | bytes 786440 | tf_op jit(solution)/shard_map/ppermute | solution.py:208
  6.5 6.4 %collective-permute-start.3 = (bf16[64,2048]{1,0:T(8,128)(2,1)}, bf16[64,2048]{1,0:T(8,128)(2,1)S(1)}, u32[]{:S(2)}, u32[]{:S(2)}) collective-permute-start(bf16[64,2048]{1,0:T(8,128)(2,1)} %refs_2_.1), channel_id=1, source_target_pairs={{0,1},{1,0},{2,3},{3,2},{4,5},{5,4},{6,7},{7,6},{8,9},{9,8},{10,11... | collective-permute-start | bytes 786440 | tf_op jit(solution)/shard_map/ppermute | solution.py:222
  6.5 11.8 %collective-permute-start.8 = (f32[16,4096]{1,0:T(8,128)}, f32[16,4096]{1,0:T(8,128)S(1)}, u32[]{:S(2)}, u32[]{:S(2)}) collective-permute-start(f32[16,4096]{1,0:T(8,128)} %refs_6_.1), channel_id=1, source_target_pairs={{8,0},{12,4},{0,8},{4,12},{10,2},{14,6},{2,10},{6,14},{24,16},{28,... | collective-permute-start | bytes 786440 | tf_op jit(solution)/shard_map/ppermute | solution.py:214
  8.5 7.9 %collective-permute-start = (bf16[64,2048]{1,0:T(8,128)(2,1)}, bf16[64,2048]{1,0:T(8,128)(2,1)S(1)}, u32[]{:S(2)}, u32[]{:S(2)}) collective-permute-start(bf16[64,2048]{1,0:T(8,128)(2,1)} %refs_3_.1), channel_id=1, source_target_pairs={{2,0},{0,2},{3,1},{1,3},{6,4},{4,6},{7,5},{5,7},{10,8},{8,10},{11,... | collective-permute-start | bytes 786440 | tf_op jit(solution)/shard_map/ppermute | solution.py:225
  9.1 0.9 %copy-start = (bf16[64,2048]{1,0:T(8,128)(2,1)S(1)}, bf16[64,2048]{1,0:T(8,128)(2,1)}, u32[]{:S(2)}) copy-start(bf16[64,2048]{1,0:T(8,128)(2,1)} %refs_2_.1) | copy-start | bytes 786436
  10.0 0.9 %copy-start.1 = (bf16[64,2048]{1,0:T(8,128)(2,1)S(1)}, bf16[64,2048]{1,0:T(8,128)(2,1)}, u32[]{:S(2)}) copy-start(bf16[64,2048]{1,0:T(8,128)(2,1)} %refs_3_.1) | copy-start | bytes 786436
  12.8 2.2 %copy-start.6 = (bf16[128,8192]{1,0:T(8,128)(2,1)S(1)}, bf16[128,8192]{1,0:T(8,128)(2,1)}, u32[]{:S(2)}) copy-start(bf16[128,8192]{1,0:T(8,128)(2,1)} %refs_1_.1) | copy-start | bytes 6291460
  12.9 5.5 %collective-permute-start.4 = (bf16[64,2048]{1,0:T(8,128)(2,1)S(1)}, bf16[64,2048]{1,0:T(8,128)(2,1)S(1)}, u32[]{:S(2)}, u32[]{:S(2)}) collective-permute-start(bf16[64,2048]{1,0:T(8,128)(2,1)S(1)} %collective-permute-done.1.refs_1_), channel_id=1, source_target_pairs={{0,1},{1,0},{2,3},{3,2},{4,5},{5,4},{6,7},{7,6},{8,9},{9,8},{10,11... | collective-permute-start | bytes 786440 | tf_op jit(solution)/shard_map/ppermute | solution.py:222
  15.0 2.0 %copy-start.2 = (bf16[64,2048]{1,0:T(8,128)(2,1)S(1)}, bf16[64,2048]{1,0:T(8,128)(2,1)}, u32[]{:S(2)}) copy-start(bf16[64,2048]{1,0:T(8,128)(2,1)} %refs_3_.1) | copy-start | bytes 786436
  15.0 3.7 %copy-start.3 = (f32[16,4096]{1,0:T(8,128)S(1)}, f32[16,4096]{1,0:T(8,128)}, u32[]{:S(2)}) copy-start(f32[16,4096]{1,0:T(8,128)} %refs_6_.1) | copy-start | bytes 786436
  15.0 3.7 %copy-start.4 = (s32[1,128]{1,0:T(1,128)S(1)}, s32[1,128]{1,0:T(1,128)}, u32[]{:S(2)}) copy-start(s32[1,128]{1,0:T(1,128)} %refs_11_.1) | copy-start | bytes 1540
  15.0 3.7 %copy-start.5 = (s32[1,128]{1,0:T(1,128)S(1)}, s32[1,128]{1,0:T(1,128)}, u32[]{:S(2)}) copy-start(s32[1,128]{1,0:T(1,128)} %refs_12_.1) | copy-start | bytes 1540
  16.4 2.0 %collective-permute-start.5 = (bf16[64,2048]{1,0:T(8,128)(2,1)S(1)}, bf16[64,2048]{1,0:T(8,128)(2,1)S(1)}, u32[]{:S(2)}, u32[]{:S(2)}) collective-permute-start(bf16[64,2048]{1,0:T(8,128)(2,1)S(1)} %collective-permute-done.refs_1_), channel_id=1, source_target_pairs={{0,1},{1,0},{2,3},{3,2},{4,5},{5,4},{6,7},{7,6},{8,9},{9,8},{10,11... | collective-permute-start | bytes 786440 | tf_op jit(solution)/shard_map/ppermute | solution.py:222
  16.8 1.6 %collective-permute-start.7 = (f32[16,4096]{1,0:T(8,128)S(1)}, f32[16,4096]{1,0:T(8,128)S(1)}, u32[]{:S(2)}, u32[]{:S(2)}) collective-permute-start(f32[16,4096]{1,0:T(8,128)S(1)} %collective-permute-done.2.refs_7_), channel_id=1, source_target_pairs={{0,1},{1,0},{2,3},{3,2},{4,5},{5,4},{6,7},{7,6},{8,9},{9,8},{10,11... | collective-permute-start | bytes 786440 | tf_op jit(solution)/shard_map/ppermute | solution.py:222
  17.0 1.8 %collective-permute-start.6 = (bf16[64,2048]{1,0:T(8,128)(2,1)S(1)}, bf16[64,2048]{1,0:T(8,128)(2,1)S(1)}, u32[]{:S(2)}, u32[]{:S(2)}) collective-permute-start(bf16[64,2048]{1,0:T(8,128)(2,1)S(1)} %copy-done.2), channel_id=1, source_target_pairs={{0,1},{1,0},{2,3},{3,2},{4,5},{5,4},{6,7},{7,6},{8,9},{9,8},{10,11... | collective-permute-start | bytes 786440 | tf_op jit(solution)/shard_map/ppermute | solution.py:222
  18.4 2.0 %collective-permute-start.9 = (f32[16,4096]{1,0:T(8,128)S(1)}, f32[16,4096]{1,0:T(8,128)S(1)}, u32[]{:S(2)}, u32[]{:S(2)}) collective-permute-start(f32[16,4096]{1,0:T(8,128)S(1)} %collective-permute-done.8.here_ref), channel_id=1, source_target_pairs={{0,1},{1,0},{2,3},{3,2},{4,5},{5,4},{6,7},{7,6},{8,9},{9,8},{10,11... | collective-permute-start | bytes 786440 | tf_op jit(solution)/shard_map/ppermute | solution.py:222

commit v6 on v5

--- a/solution.py
+++ b/solution.py
@@ -254,9 +254,9 @@
     fetched = first + fetched[len(first) :]
     others_in = [to_core(a) for a in far_in]
     other_out = to_core(late_out)
-    (in_sum,) = project(
-        [(activations, far_in + [to_core(proj_in)], far_own + [1])], table, [in_sum]
-    )
+    (in_sum,) = project([(activations, far_in, far_own)], table, [in_sum])
+    in_sum, other_in = after(in_sum, to_core(proj_in))
+    others_in = others_in + [other_in]
     if on_line:
         beside, across = fetched
         beside_other = to_core(beside)
@@ -271,7 +271,7 @@
         ]
         for array, places in (
             (out_grads, far_own),
-            (activations, far_other),
+            (activations, far_other + [1]),
             (out_grads, far_other + [1]),
         )
     ]

time: 21.5 us -> 21.1 us (0.981)
  Pallas kernels: 6.68 us -> 5.86 us
  local copies, waits for them, and re-layouts: 3.24 us -> 3.6 us
    pallas_call x2, Pallas kernels: 3.86 us -> 3.34 us  [project(): pl.pallas_call(kernel, out_shape=shapes, in_specs=[ANY] * n + [VMEM] * (t...]
    pallas_call x1, Pallas kernels: 1.62 us -> 1.32 us  [gradients(): pl.pallas_call(kernel, out_shape=(jax.ShapeDtypeStruct((2 * TRAJ_DEV, fla...]
    dynamic_slice x1, local copies, waits for them, and re-layouts: 1.31 us -> 1.59 us  [body(): lax.dynamic_slice_in_dim(array, chunk[place] * width, width, 1)]
    ppermute x1, waiting for transfers between devices: 0.79 us -> 1.03 us  [fetch_queries(): lax.ppermute(queries, ('traj', 'sub'), [(2 * ((z + 2) % n), 2 * z) for z...]
  transfers between devices with their start and end apart: 10 -> 10, of which waited for: 2 -> 2; matrix products, arithmetic and copies ran while one was open for 6% -> 8% of each run, Pallas kernels for 27% -> 24%
where the time goes in v6:
time: 21.1 us; the launch traced here: 20.8 us
  starting transfers between devices  9.98 us (47%)
  Pallas kernels  5.86 us (28%)
  local copies, waits for them, and re-layouts  3.6 us (17%)
  waiting for transfers between devices  1.26 us (6%)
    ppermute x1, starting transfers between devices, fetch_queries(): lax.ppermute(queries, ('traj', 'sub'), [(2 * ((z + 1) % n), 2 * z) for z...  3.6 us
    ppermute x2, starting transfers between devices, from_chip(): return lax.ppermute(a, 'fsdp', [((i + d) % chips, i) for i in range(chips)])  3.54 us
    pallas_call x2, Pallas kernels, project(): pl.pallas_call(kernel, out_shape=shapes, in_specs=[ANY] * n + [VMEM] * (t...  3.34 us
    unnamed x14, local copies, waits for them, and re-layouts  2 us
    ppermute x1, starting transfers between devices, fetch_queries(): lax.ppermute(queries, ('traj', 'sub'), [(2 * ((z + 2) % n), 2 * z) for z...  1.91 us
    dynamic_slice x1, local copies, waits for them, and re-layouts, body(): lax.dynamic_slice_in_dim(array, chunk[place] * width, width, 1)  1.59 us
    pallas_call x1, Pallas kernels, gradients(): pl.pallas_call(kernel, out_shape=(jax.ShapeDtypeStruct((2 * TRAJ_DEV, fla...  1.32 us
    ppermute x1, waiting for transfers between devices, fetch_queries(): lax.ppermute(queries, ('traj', 'sub'), [(2 * ((z + 2) % n), 2 * z) for z...  1.03 us
  transfers between devices with their start and end apart: 10, of which 2 were waited for; matrix products, arithmetic and copies ran while one was open for 8% of the time, Pallas kernels for 24%

profile of v6, /device:TPU:0, one launch (start us, length us, event | category | flops | bytes accessed | tf_op | source)
XLA Modules:
  0.0 20.8 jit_solution(6805306682209259487)
XLA Ops:
  0.0 2.9 %collective-permute-start.1 = (bf16[64,2048]{1,0:T(8,128)(2,1)}, bf16[64,2048]{1,0:T(8,128)(2,1)S(1)}, u32[]{:S(2)}, u32[]{:S(2)}) collective-permute-start(bf16[64,2048]{1,0:T(8,128)(2,1)} %refs_2_.1), channel_id=1, source_target_pairs={{2,0},{0,2},{3,1},{1,3},{6,4},{4,6},{7,5},{5,7},{10,8},{8,10},{11,... | collective-permute-start | bytes 786440 | tf_op jit(solution)/shard_map/ppermute | solution.py:225
  2.9 3.6 %collective-permute-start.2 = (f32[16,4096]{1,0:T(8,128)}, f32[16,4096]{1,0:T(8,128)S(1)}, u32[]{:S(2)}, u32[]{:S(2)}) collective-permute-start(f32[16,4096]{1,0:T(8,128)} %refs_8_.1), channel_id=1, source_target_pairs={{4,0},{8,4},{12,8},{0,12},{13,1},{1,5},{5,9},{9,13},{6,2},{10,6},{... | collective-permute-start | bytes 786440 | tf_op jit(solution)/shard_map/ppermute | solution.py:208
  6.5 0.0 collective-permute-start.3
  6.5 1.9 %collective-permute-start.8 = (f32[16,4096]{1,0:T(8,128)}, f32[16,4096]{1,0:T(8,128)S(1)}, u32[]{:S(2)}, u32[]{:S(2)}) collective-permute-start(f32[16,4096]{1,0:T(8,128)} %refs_8_.1), channel_id=1, source_target_pairs={{8,0},{12,4},{0,8},{4,12},{10,2},{14,6},{2,10},{6,14},{24,16},{28,... | collective-permute-start | bytes 786440 | tf_op jit(solution)/shard_map/ppermute | solution.py:214
  8.5 0.6 %collective-permute-start = (bf16[64,2048]{1,0:T(8,128)(2,1)}, bf16[64,2048]{1,0:T(8,128)(2,1)S(1)}, u32[]{:S(2)}, u32[]{:S(2)}) collective-permute-start(bf16[64,2048]{1,0:T(8,128)(2,1)} %refs_3_.1), channel_id=1, source_target_pairs={{2,0},{0,2},{3,1},{1,3},{6,4},{4,6},{7,5},{5,7},{10,8},{8,10},{11,... | collective-permute-start | bytes 786440 | tf_op jit(solution)/shard_map/ppermute | solution.py:225
  9.1 0.9 %copy-done = bf16[64,2048]{1,0:T(8,128)(2,1)S(1)} copy-done((bf16[64,2048]{1,0:T(8,128)(2,1)S(1)}, bf16[64,2048]{1,0:T(8,128)(2,1)}, u32[]{:S(2)}) %copy-start) | copy-done | bytes 262168
  10.0 0.9 %copy-done.1 = bf16[64,2048]{1,0:T(8,128)(2,1)S(1)} copy-done((bf16[64,2048]{1,0:T(8,128)(2,1)S(1)}, bf16[64,2048]{1,0:T(8,128)(2,1)}, u32[]{:S(2)}) %copy-start.1) | copy-done | bytes 262168
  11.0 1.9 %shard_map.73 = (f32[128,64]{1,0:T(8,128)S(1)}, f32[128,64]{1,0:T(8,128)S(1)}) custom-call(bf16[128,8192]{1,0:T(8,128)(2,1)} %refs_0_.3, bf16[128,8192]{1,0:T(8,128)(2,1)} %refs_1_.1, bf16[64,2048]{1,0:T(8,128)(2,1)S(1)} %copy-done, bf16[64,2048]{1,0:T(8,128)(2,1)S(1)} %copy-done.1), custom_call_target="tpu_custom_call" | custom-call | flops 1 | bytes 1 | tf_op jit(solution)/shard_map/pallas_call | solution.py:74
  12.8 0.0 copy-start.6
  12.9 0.0 collective-permute-done.1.refs_1_
  12.9 0.0 collective-permute-done.2.refs_9_
  12.9 0.1 collective-permute-start.4
  13.0 1.5 %shard_map.74.refs_11_ = f32[128,64]{1,0:T(8,128)S(1)} custom-call(bf16[128,8192]{1,0:T(8,128)(2,1)} %refs_0_.3, bf16[64,2048]{1,0:T(8,128)(2,1)S(1)} %collective-permute-done.1.refs_1_, f32[128,64]{1,0:T(8,128)S(1)} %get-tuple-element.33.refs_2_), custom_call_target="tpu_custom_call" | custom-call | flops 1 | bytes 1 | tf_op jit(solution)/shard_map/pallas_call | solution.py:74
  14.5 0.0 copy-start.2
  14.5 0.0 copy-start.3
  14.5 0.0 copy-start.4
  14.5 0.0 copy-start.5
  14.5 0.0 collective-permute-done.3.refs_5_
  14.5 0.1 copy-done.6
  14.6 1.6 %constant_dynamic-slice_fusion = (bf16[128,2048]{1,0:T(8,128)(2,1)S(1)}, bf16[128,2048]{1,0:T(8,128)(2,1)S(1)}, bf16[128,2048]{1,0:T(8,128)(2,1)S(1)}, bf16[128,2048]{1,0:T(8,128)(2,1)S(1)}, bf16[128,2048]{1,0:T(8,128)(2,1)S(1)}) fusion(bf16[128,8192]{1,0:T(8,128)(2,1)} %refs_1_.1, s32[]{:T(128)S(6)} %select_n.13, s32[]{:T(128)S(6)} %select_n.12, ...), kind=kLoop, calls=%fused_computation | loop fusion | bytes 5242892 | tf_op jit(solution)/shard_map/dynamic_slice | solution.py:269
  16.2 0.0 collective-permute-done.refs_1_
  16.2 0.3 %collective-permute-start.5 = (bf16[64,2048]{1,0:T(8,128)(2,1)S(1)}, bf16[64,2048]{1,0:T(8,128)(2,1)S(1)}, u32[]{:S(2)}, u32[]{:S(2)}) collective-permute-start(bf16[64,2048]{1,0:T(8,128)(2,1)S(1)} %collective-permute-done.refs_1_), channel_id=1, source_target_pairs={{0,1},{1,0},{2,3},{3,2},{4,5},{5,4},{6,7},{7,6},{8,9},{9,8},{10,11... | collective-permute-start | bytes 786440 | tf_op jit(solution)/shard_map/ppermute | solution.py:222
  16.6 0.2 %collective-permute-start.7 = (f32[16,4096]{1,0:T(8,128)S(1)}, f32[16,4096]{1,0:T(8,128)S(1)}, u32[]{:S(2)}, u32[]{:S(2)}) collective-permute-start(f32[16,4096]{1,0:T(8,128)S(1)} %collective-permute-done.2.refs_9_), channel_id=1, source_target_pairs={{0,1},{1,0},{2,3},{3,2},{4,5},{5,4},{6,7},{7,6},{8,9},{9,8},{10,11... | collective-permute-start | bytes 786440 | tf_op jit(solution)/shard_map/ppermute | solution.py:222
  16.8 0.3 %collective-permute-start.6 = (bf16[64,2048]{1,0:T(8,128)(2,1)S(1)}, bf16[64,2048]{1,0:T(8,128)(2,1)S(1)}, u32[]{:S(2)}, u32[]{:S(2)}) collective-permute-start(bf16[64,2048]{1,0:T(8,128)(2,1)S(1)} %copy-done.2), channel_id=1, source_target_pairs={{0,1},{1,0},{2,3},{3,2},{4,5},{5,4},{6,7},{7,6},{8,9},{9,8},{10,11... | collective-permute-start | bytes 786440 | tf_op jit(solution)/shard_map/ppermute | solution.py:222
  17.1 0.3 %shard_map.75.refs_12_ = f32[128,64]{1,0:T(8,128)S(1)} custom-call(f32[128,64]{1,0:T(8,128)S(1)} %get-tuple-element.49.base_ref, bf16[128,2048]{1,0:T(8,128)(2,1)S(1)} %get-tuple-element.50.refs_0_, bf16[64,2048]{1,0:T(8,128)(2,1)S(1)} %collective-permute-done.refs_1_), custom_call_target="tpu_custom_call" | custom-call | flops 1 | bytes 1 | tf_op jit(solution)/shard_map/pallas_call | solution.py:94
  17.4 1.0 %collective-permute-done.8.here_ref = f32[16,4096]{1,0:T(8,128)S(1)} collective-permute-done((f32[16,4096]{1,0:T(8,128)}, f32[16,4096]{1,0:T(8,128)S(1)}, u32[]{:S(2)}, u32[]{:S(2)}) %collective-permute-start.8) | collective-permute-done | bytes 262176 | tf_op jit(solution)/shard_map/ppermute | solution.py:214
  18.4 0.0 collective-permute-done.5.refs_6_
  18.4 0.0 collective-permute-done.4.refs_4_
  18.4 0.1 collective-permute-done.6.refs_7_
  18.6 1.3 %shard_map.76 = (bf16[16,4096]{1,0:T(8,128)(2,1)S(1)}, f32[8,64]{1,0:T(8,128)S(1)}) custom-call(bf16[128,2048]{1,0:T(8,128)(2,1)S(1)} %get-tuple-element.38.refs_0_, bf16[128,2048]{1,0:T(8,128)(2,1)S(1)} %get-tuple-element.39.refs_1_, bf16[128,2048]{1,0:T(8,128)(2,1)S(1)} %get-tuple-element.40.refs_2_, bf16[128,2048]{1,0:T(8,128)(2,1)S(1)} %get-tuple-element.41.refs_3_, ...), custom_call_target="tpu_custom_call" | custom-call | flops 1 | bytes 1 | tf_op jit(solution)/shard_map/pallas_call | solution.py:158
  19.9 0.0 collective-permute-done.9.there_ref
  19.9 0.9 %shard_map.77 = f32[8,64]{1,0:T(8,128)} custom-call(f32[8,64]{1,0:T(8,128)S(1)} %get-tuple-element.52.base_ref, bf16[16,4096]{1,0:T(8,128)(2,1)S(1)} %get-tuple-element.53.stack_ref, f32[16,4096]{1,0:T(8,128)S(1)} %collective-permute-done.8.here_ref, f32[16,4096]{1,0:T(8,128)S(1)} %collective-permute-done.9.there_ref), custom_call_target="tpu_custom_call" | custom-call | flops 1 | bytes 1 | tf_op jit(solution)/shard_map/pallas_call | solution.py:189
  (8 shorter events, 0.0 us)
Async XLA Ops:
  0.0 12.9 %collective-permute-start.1 = (bf16[64,2048]{1,0:T(8,128)(2,1)}, bf16[64,2048]{1,0:T(8,128)(2,1)S(1)}, u32[]{:S(2)}, u32[]{:S(2)}) collective-permute-start(bf16[64,2048]{1,0:T(8,128)(2,1)} %refs_2_.1), channel_id=1, source_target_pairs={{2,0},{0,2},{3,1},{1,3},{6,4},{4,6},{7,5},{5,7},{10,8},{8,10},{11,... | collective-permute-start | bytes 786440 | tf_op jit(solution)/shard_map/ppermute | solution.py:225
  2.9 9.9 %collective-permute-start.2 = (f32[16,4096]{1,0:T(8,128)}, f32[16,4096]{1,0:T(8,128)S(1)}, u32[]{:S(2)}, u32[]{:S(2)}) collective-permute-start(f32[16,4096]{1,0:T(8,128)} %refs_8_.1), channel_id=1, source_target_pairs={{4,0},{8,4},{12,8},{0,12},{13,1},{1,5},{5,9},{9,13},{6,2},{10,6},{... | collective-permute-start | bytes 786440 | tf_op jit(solution)/shard_map/ppermute | solution.py:208
  6.5 8.0 %collective-permute-start.3 = (bf16[64,2048]{1,0:T(8,128)(2,1)}, bf16[64,2048]{1,0:T(8,128)(2,1)S(1)}, u32[]{:S(2)}, u32[]{:S(2)}) collective-permute-start(bf16[64,2048]{1,0:T(8,128)(2,1)} %refs_2_.1), channel_id=1, source_target_pairs={{0,1},{1,0},{2,3},{3,2},{4,5},{5,4},{6,7},{7,6},{8,9},{9,8},{10,11... | collective-permute-start | bytes 786440 | tf_op jit(solution)/shard_map/ppermute | solution.py:222
  6.5 11.8 %collective-permute-start.8 = (f32[16,4096]{1,0:T(8,128)}, f32[16,4096]{1,0:T(8,128)S(1)}, u32[]{:S(2)}, u32[]{:S(2)}) collective-permute-start(f32[16,4096]{1,0:T(8,128)} %refs_8_.1), channel_id=1, source_target_pairs={{8,0},{12,4},{0,8},{4,12},{10,2},{14,6},{2,10},{6,14},{24,16},{28,... | collective-permute-start | bytes 786440 | tf_op jit(solution)/shard_map/ppermute | solution.py:214
  8.5 7.7 %collective-permute-start = (bf16[64,2048]{1,0:T(8,128)(2,1)}, bf16[64,2048]{1,0:T(8,128)(2,1)S(1)}, u32[]{:S(2)}, u32[]{:S(2)}) collective-permute-start(bf16[64,2048]{1,0:T(8,128)(2,1)} %refs_3_.1), channel_id=1, source_target_pairs={{2,0},{0,2},{3,1},{1,3},{6,4},{4,6},{7,5},{5,7},{10,8},{8,10},{11,... | collective-permute-start | bytes 786440 | tf_op jit(solution)/shard_map/ppermute | solution.py:225
  9.1 0.9 %copy-start = (bf16[64,2048]{1,0:T(8,128)(2,1)S(1)}, bf16[64,2048]{1,0:T(8,128)(2,1)}, u32[]{:S(2)}) copy-start(bf16[64,2048]{1,0:T(8,128)(2,1)} %refs_2_.1) | copy-start | bytes 786436
  10.0 0.9 %copy-start.1 = (bf16[64,2048]{1,0:T(8,128)(2,1)S(1)}, bf16[64,2048]{1,0:T(8,128)(2,1)}, u32[]{:S(2)}) copy-start(bf16[64,2048]{1,0:T(8,128)(2,1)} %refs_3_.1) | copy-start | bytes 786436
  12.8 1.8 %copy-start.6 = (bf16[128,8192]{1,0:T(8,128)(2,1)S(1)}, bf16[128,8192]{1,0:T(8,128)(2,1)}, u32[]{:S(2)}) copy-start(bf16[128,8192]{1,0:T(8,128)(2,1)} %refs_0_.3) | copy-start | bytes 6291460
  12.9 5.5 %collective-permute-start.4 = (bf16[64,2048]{1,0:T(8,128)(2,1)S(1)}, bf16[64,2048]{1,0:T(8,128)(2,1)S(1)}, u32[]{:S(2)}, u32[]{:S(2)}) collective-permute-start(bf16[64,2048]{1,0:T(8,128)(2,1)S(1)} %collective-permute-done.1.refs_1_), channel_id=1, source_target_pairs={{0,1},{1,0},{2,3},{3,2},{4,5},{5,4},{6,7},{7,6},{8,9},{9,8},{10,11... | collective-permute-start | bytes 786440 | tf_op jit(solution)/shard_map/ppermute | solution.py:222
  14.5 2.3 %copy-start.2 = (bf16[64,2048]{1,0:T(8,128)(2,1)S(1)}, bf16[64,2048]{1,0:T(8,128)(2,1)}, u32[]{:S(2)}) copy-start(bf16[64,2048]{1,0:T(8,128)(2,1)} %refs_3_.1) | copy-start | bytes 786436
  14.5 4.1 %copy-start.3 = (f32[16,4096]{1,0:T(8,128)S(1)}, f32[16,4096]{1,0:T(8,128)}, u32[]{:S(2)}) copy-start(f32[16,4096]{1,0:T(8,128)} %refs_8_.1) | copy-start | bytes 786436
  14.5 4.1 %copy-start.4 = (s32[1,128]{1,0:T(1,128)S(1)}, s32[1,128]{1,0:T(1,128)}, u32[]{:S(2)}) copy-start(s32[1,128]{1,0:T(1,128)} %refs_13_.1) | copy-start | bytes 1540
  14.5 4.1 %copy-start.5 = (s32[1,128]{1,0:T(1,128)S(1)}, s32[1,128]{1,0:T(1,128)}, u32[]{:S(2)}) copy-start(s32[1,128]{1,0:T(1,128)} %refs_14_.1) | copy-start | bytes 1540
  16.2 2.2 %collective-permute-start.5 = (bf16[64,2048]{1,0:T(8,128)(2,1)S(1)}, bf16[64,2048]{1,0:T(8,128)(2,1)S(1)}, u32[]{:S(2)}, u32[]{:S(2)}) collective-permute-start(bf16[64,2048]{1,0:T(8,128)(2,1)S(1)} %collective-permute-done.refs_1_), channel_id=1, source_target_pairs={{0,1},{1,0},{2,3},{3,2},{4,5},{5,4},{6,7},{7,6},{8,9},{9,8},{10,11... | collective-permute-start | bytes 786440 | tf_op jit(solution)/shard_map/ppermute | solution.py:222
  16.6 1.9 %collective-permute-start.7 = (f32[16,4096]{1,0:T(8,128)S(1)}, f32[16,4096]{1,0:T(8,128)S(1)}, u32[]{:S(2)}, u32[]{:S(2)}) collective-permute-start(f32[16,4096]{1,0:T(8,128)S(1)} %collective-permute-done.2.refs_9_), channel_id=1, source_target_pairs={{0,1},{1,0},{2,3},{3,2},{4,5},{5,4},{6,7},{7,6},{8,9},{9,8},{10,11... | collective-permute-start | bytes 786440 | tf_op jit(solution)/shard_map/ppermute | solution.py:222
  16.8 1.8 %collective-permute-start.6 = (bf16[64,2048]{1,0:T(8,128)(2,1)S(1)}, bf16[64,2048]{1,0:T(8,128)(2,1)S(1)}, u32[]{:S(2)}, u32[]{:S(2)}) collective-permute-start(bf16[64,2048]{1,0:T(8,128)(2,1)S(1)} %copy-done.2), channel_id=1, source_target_pairs={{0,1},{1,0},{2,3},{3,2},{4,5},{5,4},{6,7},{7,6},{8,9},{9,8},{10,11... | collective-permute-start | bytes 786440 | tf_op jit(solution)/shard_map/ppermute | solution.py:222
  18.4 1.5 %collective-permute-start.9 = (f32[16,4096]{1,0:T(8,128)S(1)}, f32[16,4096]{1,0:T(8,128)S(1)}, u32[]{:S(2)}, u32[]{:S(2)}) collective-permute-start(f32[16,4096]{1,0:T(8,128)S(1)} %collective-permute-done.8.here_ref), channel_id=1, source_target_pairs={{0,1},{1,0},{2,3},{3,2},{4,5},{5,4},{6,7},{7,6},{8,9},{9,8},{10,11... | collective-permute-start | bytes 786440 | tf_op jit(solution)/shard_map/ppermute | solution.py:222
